TPU v7x, 512 devices: a whole 4x8x8 slice. The times are simulated.
512 devices in a mesh: site: 32 (over x, z), sp: 16 (over y, core).
Axes of the slice: x: 4, y: 8, z: 8, core: 2. Of those that a mesh axis runs over, the one named last changes fastest.
Arguments:
- presence: int32 [114688, 2048], P('site', 'sp'), may hold values 0 or 1
- utility_noise: bfloat16 [114688, 2048], P('site', 'sp'), may hold values from -5 to 5
- factors: float32 [16, 114688], P(None, 'site'), may hold values from -6 to 6
- loadings: float32 [16, 2048], P(None, 'sp'), may hold values from -0.3 to 0.3
- loading_precision: float32 [16, 2048], P(None, 'sp'), may hold values from 0.5 to 229376
- neighbours: int32 [15, 114688], P(None, 'site'), may hold values from -1 to 114686, as said below
- neighbour_weights: float32 [15, 114688], P(None, 'site'), may hold values from 0 to 0.1
- conditional_variance: float32 [114688], P('site'), may hold values from 0.1 to 1
- factor_noise: float32 [16, 114688], P(None, 'site'), may hold values from -5 to 5
Outputs:
- utilities: bfloat16 [114688, 2048], P('site', 'sp')
- new_loadings: float32 [16, 2048], P(None, 'sp')
- new_factors: float32 [16, 114688], P(None, 'site')
Inputs may be any that keep to these rules, and one draw needn't show every extreme that they name: The k-th neighbour of site i (k from 0) is i - o with k * 96 + 1 <= o <= (k + 1) * 96, or -1 where that index would be negative; so all neighbours of a site are distinct, earlier, and at most 1440 sites before it. Every seventh site's last neighbour, where it is not -1, lies exactly 1440 sites before it, and the last site's first neighbour is the site just before it.
All inputs are finite; a program needn't handle non-finite values. No bound on the sum of `presence` on one device may be relied on, other than what follows from the above.
Results may differ from a plain program's by a relative error of at most 0.001.
Values sent between devices are 32-bit elements; how exact they have to be, the bound alone decides.
A program may use at most 128 MiB of HBM per device.

v0:
```python
import jax
import jax.numpy as jnp
from jax import lax
from jax.sharding import PartitionSpec as P

REACH = 1440


HIGH = lax.Precision.HIGHEST
inv_root_two_pi = 0.3989422804014327
inv_root_two = 0.7071067811865476


def from_behind(shard, axis, by):
    length = lax.axis_size(axis)
    pairs = [(i, i + by) for i in range(length) if 0 <= i + by < length]
    return lax.ppermute(shard, axis, pairs)


def utilities_block(eta_block, loadings, presence, noise):
    mean = lax.dot_general(
        eta_block,
        loadings,
        (((0,), (0,)), ((), ())),
        precision=HIGH,
        preferred_element_type=jnp.float32,
    )
    signs = (2 * presence - 1).astype(jnp.float32)
    shifted = signs * mean
    ratio = (
        jnp.exp(-0.5 * shifted * shifted)
        * inv_root_two_pi
        / (0.5 * lax.erfc(-shifted * inv_root_two))
    )
    spread = 1.0 - ratio * (ratio + shifted)
    return mean + signs * ratio + jnp.sqrt(spread) * noise.astype(jnp.float32)


def cholesky_solve(base, extra, rhs, noise):
    count = base.shape[0]
    lower = {}
    for j in range(count):
        accum = base[j, j] + extra[j]
        for k in range(j):
            accum = accum - lower[j, k] * lower[j, k]
        pivot = jnp.sqrt(accum)
        lower[j, j] = pivot
        for i in range(j + 1, count):
            accum = base[i, j] + jnp.zeros_like(pivot)
            for k in range(j):
                accum = accum - lower[i, k] * lower[j, k]
            lower[i, j] = accum / pivot
    middle = []
    for i in range(count):
        accum = rhs[i]
        for k in range(i):
            accum = accum - lower[i, k] * middle[k]
        value = accum / lower[i, i]
        if noise is not None:
            value = value + noise[i]
        middle.append(value)
    result = [None] * count
    for i in range(count - 1, -1, -1):
        accum = middle[i]
        for k in range(i + 1, count):
            accum = accum - lower[k, i] * result[k]
        result[i] = accum / lower[i, i]
    return jnp.stack(result, axis=0)


def prior_mean(window, ids, weights, anchor):
    local = ids - anchor
    valid = ids >= 0
    local = jnp.where(valid, local, 0)
    picked = jnp.take(window, local, axis=1)
    scaled = jnp.where(valid, weights, jnp.float32(0.0))
    return jnp.sum(picked * scaled[None, :, :], axis=1)


def site_update(lgram, variance, pull, prior, noise):
    inverse = 1.0 / variance
    extra = jnp.broadcast_to(inverse[None, :], pull.shape)
    return cholesky_solve(lgram, extra, pull + prior * inverse[None, :], noise)


def shards(
    presence,
    utility_noise,
    factors,
    loadings,
    loading_precision,
    neighbours,
    neighbour_weights,
    conditional_variance,
    factor_noise,
):
    rows = factors.shape[1]
    rim = from_behind(factors[:, rows - REACH :], "site", 1)
    window = jnp.concatenate([rim, factors], axis=1)
    anchor = lax.axis_index("site") * rows - REACH
    draw = utilities_block(factors, loadings, presence, utility_noise)
    cross = jnp.dot(factors, draw, precision=HIGH, preferred_element_type=jnp.float32)
    gram = jnp.dot(factors, factors.T, precision=HIGH, preferred_element_type=jnp.float32)
    cross, gram = lax.psum((cross, gram), "site")
    new_loadings = cholesky_solve(gram, loading_precision, cross, None)
    pull = lax.dot_general(
        new_loadings,
        draw,
        (((1,), (1,)), ((), ())),
        precision=HIGH,
        preferred_element_type=jnp.float32,
    )
    lgram_part = jnp.dot(
        new_loadings, new_loadings.T, precision=HIGH, preferred_element_type=jnp.float32
    )
    pull, lgram = lax.psum((pull, lgram_part), "sp")
    prior = prior_mean(window, neighbours, neighbour_weights, anchor)
    new_factors = site_update(lgram, conditional_variance, pull, prior, factor_noise)
    return (draw.astype(jnp.bfloat16), new_loadings, new_factors)


def solution(mesh):
    in_specs = (
        P("site", "sp"),
        P("site", "sp"),
        P(None, "site"),
        P(None, "sp"),
        P(None, "sp"),
        P(None, "site"),
        P(None, "site"),
        P("site"),
        P(None, "site"),
    )
    out_specs = (P("site", "sp"), P(None, "sp"), P(None, "site"))
    return jax.shard_map(shards, mesh=mesh, in_specs=in_specs, out_specs=out_specs, check_vma=False)
```

profile of v0, /device:TPU:1, one launch (start us, length us, event | category | flops | bytes accessed | tf_op | source)
XLA Modules:
  0.0 1757.9 jit_solution(3046021093028674490)
XLA Ops:
  8.7 10.4 fusion.136
  20.2 122.3 %all-reduce = (f32[16,16]{1,0:T(8,128)S(1)}, f32[16,128]{1,0:T(8,128)S(1)}) all-reduce(f32[16,16]{1,0:T(8,128)S(1)} %fusion.137, f32[16,128]{1,0:T(8,128)S(1)} %convolution_bitcast_fusion), channel_id=1, replica_groups=mesh['site'=32,'sp'=16] {'site'}, use_global_device_ids=true, to_apply=%region_1.0 | all-reduce | flops 2304 | bytes 18432 | tf_op jit(solution)/shard_map/psum | solution.py:104
  148.3 75.3 %subtract_divide_fusion.158 = (f32[1,128]{1,0:T(1,128)S(1)}, f32[1,128]{1,0:T(1,128)S(1)}, f32[1,128]{1,0:T(1,128)S(1)}, f32[1,128]{1,0:T(1,128)S(1)}, f32[1,128...) fusion(f32[16,128]{1,0:T(8,128)S(1)} %get-tuple-element.36, ...), kind=kLoop, calls=%fused_computation.450 | loop fusion | flops 187520 | bytes 83936 | tf_op jit(solution)/shard_map/div | solution.py:58
  223.6 74.6 %subtract_divide_fusion.291 = (f32[128]{0:T(128)S(1)}, f32[128]{0:T(128)S(1)}, f32[128]{0:T(128)S(1)}, f32[128]{0:T(128)S(1)}, f32[128]{0:T(128)S(1)}, /*index=5...) fusion(f32[16,128]{1,0:T(8,128)S(1)} %get-tuple-element.36, ...), kind=kLoop, calls=%fused_computation.600 | loop fusion | flops 187392 | bytes 83420 | tf_op jit(solution)/shard_map/div | solution.py:58
  298.2 10.7 subtract_divide_fusion.277
  311.1 10.7 subtract_divide_fusion.144
  327.8 64.7 %psum.31 = f32[16,16]{1,0:T(8,128)S(1)} all-reduce(f32[16,16]{1,0:T(8,128)S(1)} %fusion.139), channel_id=1, replica_groups=mesh['site'=32,'sp'=16] {'sp'}, use_global_device_ids=true, to_apply=%region_4.5 | all-reduce | flops 256 | bytes 2048 | tf_op jit(solution)/shard_map/psum | solution.py:116
  398.2 86.7 %subtract_divide_fusion.15 = (f32[3584]{0:T(1024)}, f32[3584]{0:T(1024)S(1)}, f32[3584]{0:T(1024)S(1)}, f32[3584]{0:T(1024)S(1)}, f32[3584]{0:T(1024)S(1)}, /*in...) fusion(f32[]{:T(128)} %bitcast.308, ...), kind=kLoop, calls=%fused_computation.56 | loop fusion | flops 5254144 | bytes 688668 | tf_op jit(solution)/shard_map/div | solution.py:52
  491.3 9.5 subtract_divide_fusion.35
  500.8 13.3 subtract_divide_fusion.34
  514.1 17.7 %subtract_divide_fusion.33 = f32[3584]{0:T(1024)} fusion(f32[3584]{0:T(1024)S(1)} %get-tuple-element.83, f32[3584]{0:T(1024)S(1)} %get-tuple-element.63, f32[3584]{0:T(1024)S(1)} %get-tuple-element.84, f32[3584]{0:T(1024)S(1)} %get-tuple-element.64, f32[3584]{0:T(1024)S(1)} %get-tuple-element.85, f32[3584]{0:T(1024)S(1)} %get-tuple-element.65, ...), kind=kLoop, calls=%fused_computation.83 | loop fusion | flops 860160 | bytes 315500 | tf_op jit(solution)/shard_map/div | solution.py:52
  531.8 22.9 %subtract_divide_fusion.32 = f32[3584]{0:T(1024)} fusion(f32[3584]{0:T(1024)S(1)} %get-tuple-element.83, f32[3584]{0:T(1024)S(1)} %get-tuple-element.67, f32[3584]{0:T(1024)S(1)} %get-tuple-element.84, f32[3584]{0:T(1024)S(1)} %get-tuple-element.68, f32[3584]{0:T(1024)S(1)} %get-tuple-element.85, f32[3584]{0:T(1024)S(1)} %get-tuple-element.69, ...), kind=kLoop, calls=%fused_computation.82 | loop fusion | flops 1254400 | bytes 372876 | tf_op jit(solution)/shard_map/div | solution.py:52
  554.7 28.7 %subtract_divide_fusion.31 = f32[3584]{0:T(1024)} fusion(f32[3584]{0:T(1024)S(1)} %get-tuple-element.83, f32[3584]{0:T(1024)S(1)} %get-tuple-element.71, f32[3584]{0:T(1024)S(1)} %get-tuple-element.84, f32[3584]{0:T(1024)S(1)} %get-tuple-element.72, f32[3584]{0:T(1024)S(1)} %get-tuple-element.85, f32[3584]{0:T(1024)S(1)} %get-tuple-element.73, ...), kind=kLoop, calls=%fused_computation.81 | loop fusion | flops 1738240 | bytes 430256 | tf_op jit(solution)/shard_map/div | solution.py:52
  583.4 34.8 %subtract_divide_fusion.30 = f32[3584]{0:T(1024)} fusion(f32[3584]{0:T(1024)S(1)} %get-tuple-element.83, f32[3584]{0:T(1024)S(1)} %get-tuple-element.75, f32[3584]{0:T(1024)S(1)} %get-tuple-element.84, f32[3584]{0:T(1024)S(1)} %get-tuple-element.76, f32[3584]{0:T(1024)S(1)} %get-tuple-element.85, f32[3584]{0:T(1024)S(1)} %get-tuple-element.77, ...), kind=kLoop, calls=%fused_computation.80 | loop fusion | flops 2318848 | bytes 487640 | tf_op jit(solution)/shard_map/div | solution.py:52
  618.2 43.0 %subtract_sqrt_fusion.1 = f32[3584]{0:T(1024)} fusion(f32[3584]{0:T(1024)S(1)} %get-tuple-element.83, f32[3584]{0:T(1024)S(1)} %get-tuple-element.84, f32[3584]{0:T(1024)S(1)} %get-tuple-element.85, f32[3584]{0:T(1024)S(1)} %get-tuple-element.86, f32[3584]{0:T(1024)S(1)} %get-tuple-element.79, f32[3584]{0:T(1024)S(1)} %get-tuple-element.80, ...), kind=kLoop, calls=%fused_computation.74 | loop fusion | flops 3107328 | bytes 545032 | tf_op jit(solution)/shard_map/sqrt | solution.py:46
  661.2 42.4 %subtract_divide_fusion.29 = f32[3584]{0:T(1024)} fusion(f32[3584]{0:T(1024)S(1)} %get-tuple-element.83, f32[3584]{0:T(1024)S(1)} %get-tuple-element.79, f32[3584]{0:T(1024)S(1)} %get-tuple-element.84, f32[3584]{0:T(1024)S(1)} %get-tuple-element.80, f32[3584]{0:T(1024)S(1)} %get-tuple-element.85, f32[3584]{0:T(1024)S(1)} %get-tuple-element.81, ...), kind=kLoop, calls=%fused_computation.79 | loop fusion | flops 3003392 | bytes 545028 | tf_op jit(solution)/shard_map/div | solution.py:52
  703.6 35.4 %subtract_sqrt_fusion.2 = f32[3584]{0:T(1024)} fusion(f32[3584]{0:T(1024)S(1)} %get-tuple-element.79, f32[3584]{0:T(1024)S(1)} %get-tuple-element.80, f32[3584]{0:T(1024)S(1)} %get-tuple-element.81, f32[3584]{0:T(1024)S(1)} %get-tuple-element.82, f32[3584]{0:T(1024)S(1)} %get-tuple-element.75, f32[3584]{0:T(1024)S(1)} %get-tuple-element.76, ...), kind=kLoop, calls=%fused_computation.93 | loop fusion | flops 2415616 | bytes 487644 | tf_op jit(solution)/shard_map/sqrt | solution.py:46
  739.0 34.8 %subtract_divide_fusion.42 = f32[3584]{0:T(1024)} fusion(f32[3584]{0:T(1024)S(1)} %get-tuple-element.75, f32[3584]{0:T(1024)S(1)} %get-tuple-element.76, f32[3584]{0:T(1024)S(1)} %get-tuple-element.77, f32[3584]{0:T(1024)S(1)} %get-tuple-element.78, f32[3584]{0:T(1024)S(1)} %get-tuple-element.67, f32[3584]{0:T(1024)S(1)} %get-tuple-element.68, ...), kind=kLoop, calls=%fused_computation.94 | loop fusion | flops 2318848 | bytes 487640 | tf_op jit(solution)/shard_map/div | solution.py:52
  773.8 28.6 %subtract_divide_fusion.43 = f32[3584]{0:T(1024)} fusion(f32[3584]{0:T(1024)S(1)} %get-tuple-element.79, f32[3584]{0:T(1024)S(1)} %get-tuple-element.71, f32[3584]{0:T(1024)S(1)} %get-tuple-element.80, f32[3584]{0:T(1024)S(1)} %get-tuple-element.72, f32[3584]{0:T(1024)S(1)} %get-tuple-element.81, f32[3584]{0:T(1024)S(1)} %get-tuple-element.73, ...), kind=kLoop, calls=%fused_computation.95 | loop fusion | flops 1738240 | bytes 430256 | tf_op jit(solution)/shard_map/div | solution.py:52
  802.5 22.8 %subtract_divide_fusion.44 = f32[3584]{0:T(1024)} fusion(f32[3584]{0:T(1024)S(1)} %get-tuple-element.79, f32[3584]{0:T(1024)S(1)} %get-tuple-element.67, f32[3584]{0:T(1024)S(1)} %get-tuple-element.80, f32[3584]{0:T(1024)S(1)} %get-tuple-element.68, f32[3584]{0:T(1024)S(1)} %get-tuple-element.81, f32[3584]{0:T(1024)S(1)} %get-tuple-element.69, ...), kind=kLoop, calls=%fused_computation.96 | loop fusion | flops 1254400 | bytes 372876 | tf_op jit(solution)/shard_map/div | solution.py:52
  825.3 17.6 %subtract_divide_fusion.45 = f32[3584]{0:T(1024)} fusion(f32[3584]{0:T(1024)S(1)} %get-tuple-element.79, f32[3584]{0:T(1024)S(1)} %get-tuple-element.63, f32[3584]{0:T(1024)S(1)} %get-tuple-element.80, f32[3584]{0:T(1024)S(1)} %get-tuple-element.64, f32[3584]{0:T(1024)S(1)} %get-tuple-element.81, f32[3584]{0:T(1024)S(1)} %get-tuple-element.65, ...), kind=kLoop, calls=%fused_computation.98 | loop fusion | flops 860160 | bytes 315500 | tf_op jit(solution)/shard_map/div | solution.py:52
  842.9 13.1 subtract_divide_fusion.46
  856.0 9.4 subtract_divide_fusion.47
  871.7 11.5 subtract_divide_fusion.104
  883.2 29.1 %subtract_sqrt_fusion.3 = f32[3584]{0:T(1024)} fusion(f32[3584]{0:T(1024)S(1)} %get-tuple-element.75, f32[3584]{0:T(1024)S(1)} %get-tuple-element.76, f32[3584]{0:T(1024)S(1)} %get-tuple-element.77, f32[3584]{0:T(1024)S(1)} %get-tuple-element.78, f32[3584]{0:T(1024)S(1)} %get-tuple-element.67, f32[3584]{0:T(1024)S(1)} %get-tuple-element.68, ...), kind=kLoop, calls=%fused_computation.110 | loop fusion | flops 1827840 | bytes 430260 | tf_op jit(solution)/shard_map/sqrt | solution.py:46
  912.3 28.5 %subtract_divide_fusion.54 = f32[3584]{0:T(1024)} fusion(f32[3584]{0:T(1024)S(1)} %get-tuple-element.75, f32[3584]{0:T(1024)S(1)} %get-tuple-element.71, f32[3584]{0:T(1024)S(1)} %get-tuple-element.76, f32[3584]{0:T(1024)S(1)} %get-tuple-element.72, f32[3584]{0:T(1024)S(1)} %get-tuple-element.77, f32[3584]{0:T(1024)S(1)} %get-tuple-element.73, ...), kind=kLoop, calls=%fused_computation.112 | loop fusion | flops 1738240 | bytes 430256 | tf_op jit(solution)/shard_map/div | solution.py:52
  940.9 22.8 %subtract_divide_fusion.55 = f32[3584]{0:T(1024)} fusion(f32[3584]{0:T(1024)S(1)} %get-tuple-element.75, f32[3584]{0:T(1024)S(1)} %get-tuple-element.67, f32[3584]{0:T(1024)S(1)} %get-tuple-element.76, f32[3584]{0:T(1024)S(1)} %get-tuple-element.68, f32[3584]{0:T(1024)S(1)} %get-tuple-element.77, f32[3584]{0:T(1024)S(1)} %get-tuple-element.69, ...), kind=kLoop, calls=%fused_computation.113 | loop fusion | flops 1254400 | bytes 372876 | tf_op jit(solution)/shard_map/div | solution.py:52
  963.7 17.7 %subtract_divide_fusion.56 = f32[3584]{0:T(1024)} fusion(f32[3584]{0:T(1024)S(1)} %get-tuple-element.75, f32[3584]{0:T(1024)S(1)} %get-tuple-element.63, f32[3584]{0:T(1024)S(1)} %get-tuple-element.76, f32[3584]{0:T(1024)S(1)} %get-tuple-element.64, f32[3584]{0:T(1024)S(1)} %get-tuple-element.77, f32[3584]{0:T(1024)S(1)} %get-tuple-element.65, ...), kind=kLoop, calls=%fused_computation.114 | loop fusion | flops 860160 | bytes 315500 | tf_op jit(solution)/shard_map/div | solution.py:52
  981.4 13.2 subtract_divide_fusion.57
  994.6 9.4 subtract_divide_fusion.58
  1003.9 6.4 subtract_divide_fusion.59
  1010.3 23.6 %subtract_sqrt_fusion.4 = f32[3584]{0:T(1024)} fusion(f32[3584]{0:T(1024)S(1)} %get-tuple-element.71, f32[3584]{0:T(1024)S(1)} %get-tuple-element.72, f32[3584]{0:T(1024)S(1)} %get-tuple-element.73, f32[3584]{0:T(1024)S(1)} %get-tuple-element.74, f32[3584]{0:T(1024)S(1)} %get-tuple-element.67, f32[3584]{0:T(1024)S(1)} %get-tuple-element.68, ...), kind=kLoop, calls=%fused_computation.124 | loop fusion | flops 1336832 | bytes 372880 | tf_op jit(solution)/shard_map/sqrt | solution.py:46
  1033.9 22.9 %subtract_divide_fusion.65 = f32[3584]{0:T(1024)} fusion(f32[3584]{0:T(1024)S(1)} %get-tuple-element.71, f32[3584]{0:T(1024)S(1)} %get-tuple-element.67, f32[3584]{0:T(1024)S(1)} %get-tuple-element.68, f32[3584]{0:T(1024)S(1)} %get-tuple-element.69, f32[3584]{0:T(1024)S(1)} %get-tuple-element.70, f32[3584]{0:T(1024)S(1)} %get-tuple-element.63, ...), kind=kLoop, calls=%fused_computation.125 | loop fusion | flops 1254400 | bytes 372876 | tf_op jit(solution)/shard_map/div | solution.py:52
  1056.9 17.8 %subtract_divide_fusion.66 = f32[3584]{0:T(1024)} fusion(f32[3584]{0:T(1024)S(1)} %get-tuple-element.71, f32[3584]{0:T(1024)S(1)} %get-tuple-element.63, f32[3584]{0:T(1024)S(1)} %get-tuple-element.72, f32[3584]{0:T(1024)S(1)} %get-tuple-element.64, f32[3584]{0:T(1024)S(1)} %get-tuple-element.73, f32[3584]{0:T(1024)S(1)} %get-tuple-element.65, ...), kind=kLoop, calls=%fused_computation.126 | loop fusion | flops 860160 | bytes 315500 | tf_op jit(solution)/shard_map/div | solution.py:52
  1074.7 13.3 subtract_divide_fusion.67
  1088.0 9.6 subtract_divide_fusion.68
  1097.5 6.5 subtract_divide_fusion.69
  1104.0 18.5 %subtract_sqrt_fusion.5 = f32[3584]{0:T(1024)} fusion(f32[3584]{0:T(1024)S(1)} %get-tuple-element.67, f32[3584]{0:T(1024)S(1)} %get-tuple-element.68, f32[3584]{0:T(1024)S(1)} %get-tuple-element.69, f32[3584]{0:T(1024)S(1)} %get-tuple-element.70, f32[3584]{0:T(1024)S(1)} %get-tuple-element.63, f32[3584]{0:T(1024)S(1)} %get-tuple-element.64, ...), kind=kLoop, calls=%fused_computation.139 | loop fusion | flops 935424 | bytes 315504 | tf_op jit(solution)/shard_map/sqrt | solution.py:46
  1122.5 17.8 %subtract_divide_fusion.75 = f32[3584]{0:T(1024)} fusion(f32[3584]{0:T(1024)S(1)} %get-tuple-element.67, f32[3584]{0:T(1024)S(1)} %get-tuple-element.63, f32[3584]{0:T(1024)S(1)} %get-tuple-element.68, f32[3584]{0:T(1024)S(1)} %get-tuple-element.64, f32[3584]{0:T(1024)S(1)} %get-tuple-element.69, f32[3584]{0:T(1024)S(1)} %get-tuple-element.65, ...), kind=kLoop, calls=%fused_computation.141 | loop fusion | flops 860160 | bytes 315500 | tf_op jit(solution)/shard_map/div | solution.py:52
  1140.3 13.2 subtract_divide_fusion.76
  1153.5 9.4 subtract_divide_fusion.77
  1162.9 6.4 subtract_divide_fusion.78
  1169.3 13.9 subtract_sqrt_fusion.6
  1183.3 13.3 subtract_divide_fusion.84
  1196.5 9.5 subtract_divide_fusion.85
  1212.4 10.0 subtract_sqrt_fusion.7
  1222.4 9.5 subtract_divide_fusion.92
  1231.9 6.4 subtract_divide_fusion.93
  1238.3 6.9 subtract_divide_fusion.99
  1245.2 6.5 subtract_divide_fusion.23
  1251.7 9.6 subtract_divide_fusion.22
  1261.2 13.3 subtract_divide_fusion.21
  1274.6 17.8 %subtract_divide_fusion.20 = f32[3584]{0:T(1024)} fusion(f32[3584]{0:T(1024)S(1)} %get-tuple-element.87, f32[3584]{0:T(1024)S(1)} %get-tuple-element.63, f32[3584]{0:T(1024)S(1)} %get-tuple-element.91, f32[3584]{0:T(1024)S(1)} %get-tuple-element.64, f32[3584]{0:T(1024)S(1)} %get-tuple-element.94, f32[3584]{0:T(1024)S(1)} %get-tuple-element.65, ...), kind=kLoop, calls=%fused_computation.62 | loop fusion | flops 860160 | bytes 315500 | tf_op jit(solution)/shard_map/div | solution.py:52
  1292.4 23.0 %subtract_divide_fusion.19 = f32[3584]{0:T(1024)} fusion(f32[3584]{0:T(1024)S(1)} %get-tuple-element.87, f32[3584]{0:T(1024)S(1)} %get-tuple-element.67, f32[3584]{0:T(1024)S(1)} %get-tuple-element.91, f32[3584]{0:T(1024)S(1)} %get-tuple-element.68, f32[3584]{0:T(1024)S(1)} %get-tuple-element.94, f32[3584]{0:T(1024)S(1)} %get-tuple-element.69, ...), kind=kLoop, calls=%fused_computation.61 | loop fusion | flops 1254400 | bytes 372876 | tf_op jit(solution)/shard_map/div | solution.py:52
  1315.4 28.7 %subtract_divide_fusion.18 = f32[3584]{0:T(1024)} fusion(f32[3584]{0:T(1024)S(1)} %get-tuple-element.87, f32[3584]{0:T(1024)S(1)} %get-tuple-element.71, f32[3584]{0:T(1024)S(1)} %get-tuple-element.91, f32[3584]{0:T(1024)S(1)} %get-tuple-element.72, f32[3584]{0:T(1024)S(1)} %get-tuple-element.94, f32[3584]{0:T(1024)S(1)} %get-tuple-element.73, ...), kind=kLoop, calls=%fused_computation.59 | loop fusion | flops 1738240 | bytes 430256 | tf_op jit(solution)/shard_map/div | solution.py:52
  1344.1 34.9 %subtract_divide_fusion.17 = f32[3584]{0:T(1024)} fusion(f32[3584]{0:T(1024)S(1)} %get-tuple-element.87, f32[3584]{0:T(1024)S(1)} %get-tuple-element.75, f32[3584]{0:T(1024)S(1)} %get-tuple-element.91, f32[3584]{0:T(1024)S(1)} %get-tuple-element.76, f32[3584]{0:T(1024)S(1)} %get-tuple-element.94, f32[3584]{0:T(1024)S(1)} %get-tuple-element.77, ...), kind=kLoop, calls=%fused_computation.58 | loop fusion | flops 2318848 | bytes 487640 | tf_op jit(solution)/shard_map/div | solution.py:52
  1379.0 42.4 %subtract_divide_fusion.16 = f32[3584]{0:T(1024)} fusion(f32[3584]{0:T(1024)S(1)} %get-tuple-element.87, f32[3584]{0:T(1024)S(1)} %get-tuple-element.79, f32[3584]{0:T(1024)S(1)} %get-tuple-element.91, f32[3584]{0:T(1024)S(1)} %get-tuple-element.80, f32[3584]{0:T(1024)S(1)} %get-tuple-element.94, f32[3584]{0:T(1024)S(1)} %get-tuple-element.81, ...), kind=kLoop, calls=%fused_computation.57 | loop fusion | flops 3003392 | bytes 545028 | tf_op jit(solution)/shard_map/div | solution.py:52
  1423.0 11.5 subtract_divide_fusion.28
  1434.5 50.6 %subtract_sqrt_fusion = f32[3584]{0:T(1024)} fusion(f32[3584]{0:T(1024)S(1)} %get-tuple-element.87, f32[3584]{0:T(1024)S(1)} %get-tuple-element.91, f32[3584]{0:T(1024)S(1)} %get-tuple-element.94, f32[3584]{0:T(1024)S(1)} %get-tuple-element.96, f32[3584]{0:T(1024)S(1)} %get-tuple-element.79, f32[3584]{0:T(1024)S(1)} %get-tuple-element.80, ...), kind=kLoop, calls=%fused_computation.55 | loop fusion | flops 3910144 | bytes 602424 | tf_op jit(solution)/shard_map/sqrt | solution.py:46
  1485.1 9.2 broadcast_divide_fusion
  1498.1 98.9 %gather_fusion = f32[53760,16]{1,0:T(8,128)} fusion(f32[16,5024]{0,1:T(8,128)S(1)} %copy.14, s32[54272]{0:T(1024)S(1)} %pad_clamp_fusion), kind=kCustom, calls=%fused_computation | custom fusion | bytes 7096320 | tf_op jit(solution)/shard_map/jit(_take)/gather | solution.py:75
  1597.0 21.2 %multiply_reduce_fusion = f32[3584,16]{1,0:T(8,128)S(1)} fusion(f32[15,3584,16]{2,1,0:T(8,128)} %bitcast.690, f32[15,3584]{1,0:T(8,128)} %broadcast_select_fusion, pred[15,3584]{1,0:T(8,128)(4,1)} %get-tuple-element.112), kind=kLoop, calls=%fused_computation.1 | loop fusion | flops 2523136 | bytes 3938816 | tf_op jit(solution)/shard_map/reduce_sum | solution.py:77
  1620.9 59.3 %subtract_divide_fusion = (f32[3584]{0:T(1024)S(1)}, f32[3584]{0:T(1024)S(1)}) fusion(f32[3584]{0:T(1024)S(1)} %get-tuple-element.87, f32[3584]{0:T(1024)S(1)} %get-tuple-element.83, f32[3584]{0:T(1024)S(1)} %get-tuple-element.79, f32[3584]{0:T(1024)S(1)} %get-tuple-element.75, f32[3584]{0:T(1024)S(1)} %get-tuple-element.71, f32[3584]{0:T(1024)S(1)} %get-tuple-element.67, ...), kind=kLoop, calls=%fused_computation.39 | loop fusion | flops 5974528 | bytes 1161576 | tf_op jit(solution)/shard_map/div | solution.py:67
  1680.2 59.2 %subtract_divide_fusion.2 = f32[3584]{0:T(1024)S(1)} fusion(f32[3584]{0:T(1024)S(1)} %get-tuple-element.96, f32[3584]{0:T(1024)S(1)} %get-tuple-element.86, f32[3584]{0:T(1024)S(1)} %get-tuple-element.82, f32[3584]{0:T(1024)S(1)} %get-tuple-element.78, f32[3584]{0:T(1024)S(1)} %get-tuple-element.74, f32[3584]{0:T(1024)S(1)} %get-tuple-element.70, ...), kind=kLoop, calls=%fused_computation.41 | loop fusion | flops 5759488 | bytes 1147240 | tf_op jit(solution)/shard_map/div | solution.py:67
  (163 shorter events, 59.6 us)
Async XLA Ops:
  7.2 1.5 copy-start
  7.2 1611.6 %all-reduce.3.cloned.1.call-start = ((), (), s32[]{:S(2)}) async-start(), calls=%async_computation | async-start | bytes 458752 | tf_op jit(solution)/shard_map/psum | solution.py:116
  8.7 10.4 copy-start.2
  19.1 129.2 %copy-start.56 = (f32[16,128]{1,0:T(8,128)S(1)}, f32[16,128]{1,0:T(8,128)}, u32[]{:S(2)}) copy-start(f32[16,128]{1,0:T(8,128)} %param.13) | copy-start | bytes 24580
  311.1 87.1 %copy-start.1 = (f32[3584]{0:T(1024)S(1)}, f32[3584]{0:T(1024)}, u32[]{:S(2)}) copy-start(f32[3584]{0:T(1024)} %param.16) | copy-start | bytes 43012
  323.9 161.0 %copy-start.54 = (f32[16,128]{1,0:T(8,128)}, f32[16,128]{1,0:T(8,128)S(1)}, u32[]{:S(2)}) copy-start(f32[16,128]{1,0:T(8,128)S(1)} %stack.19) | copy-start | bytes 24580
  326.4 1169.2 %collective-permute-start = (f32[16,1440]{1,0:T(8,128)S(1)}, f32[16,1440]{1,0:T(8,128)S(1)}, u32[]{:S(2)}, u32[]{:S(2)}) collective-permute-start(f32[16,1440]{1,0:T(8,128)S(1)} %slice.1195), channel_id=1, source_target_pairs={{0,16},{16,32},{32,48},{48,64},{64,80},{80,96},{96,112},{112,128},... | collective-permute-start | bytes 276488 | tf_op jit(solution)/shard_map/ppermute | solution.py:17
  485.0 1000.2 %copy-start.6 = (f32[3584]{0:T(1024)}, f32[3584]{0:T(1024)S(1)}, u32[]{:S(2)}) copy-start(f32[3584]{0:T(1024)S(1)} %get-tuple-element.93) | copy-start | bytes 43012
  1231.9 189.5 %copy-start.3 = (s32[15,3584]{1,0:T(8,128)S(1)}, s32[15,3584]{1,0:T(8,128)}, u32[]{:S(2)}) copy-start(s32[15,3584]{1,0:T(8,128)} %param.14) | copy-start | bytes 645124
  1292.4 129.8 %copy-start.8 = (f32[15,3584]{1,0:T(8,128)S(1)}, f32[15,3584]{1,0:T(8,128)}, u32[]{:S(2)}) copy-start(f32[15,3584]{1,0:T(8,128)} %param.15) | copy-start | bytes 645124
  1421.4 72.9 %copy-start.4 = (f32[16,3584]{1,0:T(8,128)S(1)}, f32[16,3584]{1,0:T(8,128)}, u32[]{:S(2)}) copy-start(f32[16,3584]{1,0:T(8,128)} %param.17) | copy-start | bytes 688132
  1618.2 0.7 copy-start.55
  1618.2 2.6 copy-start.7
  1618.2 2.6 copy-start.41
  1618.2 2.6 copy-start.42
  1618.2 2.6 copy-start.43
  1618.2 2.6 copy-start.44
  1618.2 2.6 copy-start.45
  1618.2 2.6 copy-start.46
  1619.9 119.6 %copy-start.5 = (f32[16,3584]{1,0:T(8,128)S(1)}, f32[16,3584]{1,0:T(8,128)}, u32[]{:S(2)}) copy-start(f32[16,3584]{1,0:T(8,128)} %param.17) | copy-start | bytes 688132
  1619.9 119.6 %copy-start.9 = (f32[3584]{0:T(1024)S(1)}, f32[3584]{0:T(1024)}, u32[]{:S(2)}) copy-start(f32[3584]{0:T(1024)} %subtract_sqrt_fusion.4) | copy-start | bytes 43012
  1619.9 119.6 %copy-start.10 = (f32[3584]{0:T(1024)S(1)}, f32[3584]{0:T(1024)}, u32[]{:S(2)}) copy-start(f32[3584]{0:T(1024)} %get-tuple-element.477) | copy-start | bytes 43012
  1619.9 119.6 %copy-start.11 = (f32[3584]{0:T(1024)S(1)}, f32[3584]{0:T(1024)}, u32[]{:S(2)}) copy-start(f32[3584]{0:T(1024)} %subtract_divide_fusion.34) | copy-start | bytes 43012
  1619.9 119.6 %copy-start.12 = (f32[3584]{0:T(1024)S(1)}, f32[3584]{0:T(1024)}, u32[]{:S(2)}) copy-start(f32[3584]{0:T(1024)} %subtract_divide_fusion.33) | copy-start | bytes 43012
  1619.9 119.6 %copy-start.13 = (f32[3584]{0:T(1024)S(1)}, f32[3584]{0:T(1024)}, u32[]{:S(2)}) copy-start(f32[3584]{0:T(1024)} %subtract_divide_fusion.32) | copy-start | bytes 43012
  1619.9 119.6 %copy-start.14 = (f32[3584]{0:T(1024)S(1)}, f32[3584]{0:T(1024)}, u32[]{:S(2)}) copy-start(f32[3584]{0:T(1024)} %subtract_divide_fusion.31) | copy-start | bytes 43012
  1619.9 119.6 %copy-start.15 = (f32[3584]{0:T(1024)S(1)}, f32[3584]{0:T(1024)}, u32[]{:S(2)}) copy-start(f32[3584]{0:T(1024)} %subtract_divide_fusion.30) | copy-start | bytes 43012
  1620.0 119.6 %copy-start.16 = (f32[3584]{0:T(1024)S(1)}, f32[3584]{0:T(1024)}, u32[]{:S(2)}) copy-start(f32[3584]{0:T(1024)} %subtract_sqrt_fusion.1) | copy-start | bytes 43012
  1620.0 119.6 %copy-start.17 = (f32[3584]{0:T(1024)S(1)}, f32[3584]{0:T(1024)}, u32[]{:S(2)}) copy-start(f32[3584]{0:T(1024)} %subtract_divide_fusion.29) | copy-start | bytes 43012
  1620.0 119.6 %copy-start.18 = (f32[3584]{0:T(1024)S(1)}, f32[3584]{0:T(1024)}, u32[]{:S(2)}) copy-start(f32[3584]{0:T(1024)} %subtract_sqrt_fusion.2) | copy-start | bytes 43012
  1620.0 119.6 %copy-start.19 = (f32[3584]{0:T(1024)S(1)}, f32[3584]{0:T(1024)}, u32[]{:S(2)}) copy-start(f32[3584]{0:T(1024)} %subtract_divide_fusion.42) | copy-start | bytes 43012
  1620.0 119.6 %copy-start.20 = (f32[3584]{0:T(1024)S(1)}, f32[3584]{0:T(1024)}, u32[]{:S(2)}) copy-start(f32[3584]{0:T(1024)} %subtract_divide_fusion.43) | copy-start | bytes 43012
  1620.0 119.6 %copy-start.21 = (f32[3584]{0:T(1024)S(1)}, f32[3584]{0:T(1024)}, u32[]{:S(2)}) copy-start(f32[3584]{0:T(1024)} %subtract_divide_fusion.44) | copy-start | bytes 43012
  1620.0 119.6 %copy-start.22 = (f32[3584]{0:T(1024)S(1)}, f32[3584]{0:T(1024)}, u32[]{:S(2)}) copy-start(f32[3584]{0:T(1024)} %subtract_divide_fusion.45) | copy-start | bytes 43012
  1620.0 119.6 %copy-start.23 = (f32[3584]{0:T(1024)S(1)}, f32[3584]{0:T(1024)}, u32[]{:S(2)}) copy-start(f32[3584]{0:T(1024)} %subtract_divide_fusion.46) | copy-start | bytes 43012
  1620.0 119.6 %copy-start.24 = (f32[3584]{0:T(1024)S(1)}, f32[3584]{0:T(1024)}, u32[]{:S(2)}) copy-start(f32[3584]{0:T(1024)} %subtract_sqrt_fusion.3) | copy-start | bytes 43012
  1620.0 119.6 %copy-start.25 = (f32[3584]{0:T(1024)S(1)}, f32[3584]{0:T(1024)}, u32[]{:S(2)}) copy-start(f32[3584]{0:T(1024)} %subtract_divide_fusion.54) | copy-start | bytes 43012
  1620.1 119.6 %copy-start.26 = (f32[3584]{0:T(1024)S(1)}, f32[3584]{0:T(1024)}, u32[]{:S(2)}) copy-start(f32[3584]{0:T(1024)} %subtract_divide_fusion.55) | copy-start | bytes 43012
  1620.1 119.6 %copy-start.27 = (f32[3584]{0:T(1024)S(1)}, f32[3584]{0:T(1024)}, u32[]{:S(2)}) copy-start(f32[3584]{0:T(1024)} %subtract_divide_fusion.56) | copy-start | bytes 43012
  1620.1 119.6 %copy-start.28 = (f32[3584]{0:T(1024)S(1)}, f32[3584]{0:T(1024)}, u32[]{:S(2)}) copy-start(f32[3584]{0:T(1024)} %subtract_divide_fusion.57) | copy-start | bytes 43012
  1620.1 119.6 %copy-start.29 = (f32[3584]{0:T(1024)S(1)}, f32[3584]{0:T(1024)}, u32[]{:S(2)}) copy-start(f32[3584]{0:T(1024)} %subtract_divide_fusion.65) | copy-start | bytes 43012
  1620.1 119.6 %copy-start.30 = (f32[3584]{0:T(1024)S(1)}, f32[3584]{0:T(1024)}, u32[]{:S(2)}) copy-start(f32[3584]{0:T(1024)} %subtract_divide_fusion.66) | copy-start | bytes 43012
  1620.1 119.6 %copy-start.31 = (f32[3584]{0:T(1024)S(1)}, f32[3584]{0:T(1024)}, u32[]{:S(2)}) copy-start(f32[3584]{0:T(1024)} %subtract_divide_fusion.67) | copy-start | bytes 43012
  1620.1 119.6 %copy-start.32 = (f32[3584]{0:T(1024)S(1)}, f32[3584]{0:T(1024)}, u32[]{:S(2)}) copy-start(f32[3584]{0:T(1024)} %subtract_sqrt_fusion.5) | copy-start | bytes 43012
  1620.1 119.6 %copy-start.33 = (f32[3584]{0:T(1024)S(1)}, f32[3584]{0:T(1024)}, u32[]{:S(2)}) copy-start(f32[3584]{0:T(1024)} %subtract_divide_fusion.75) | copy-start | bytes 43012
  1620.1 119.6 %copy-start.34 = (f32[3584]{0:T(1024)S(1)}, f32[3584]{0:T(1024)}, u32[]{:S(2)}) copy-start(f32[3584]{0:T(1024)} %subtract_divide_fusion.76) | copy-start | bytes 43012
  1620.1 119.6 %copy-start.35 = (f32[3584]{0:T(1024)S(1)}, f32[3584]{0:T(1024)}, u32[]{:S(2)}) copy-start(f32[3584]{0:T(1024)} %subtract_sqrt_fusion.6) | copy-start | bytes 43012
  1620.2 119.6 %copy-start.36 = (f32[3584]{0:T(1024)S(1)}, f32[3584]{0:T(1024)}, u32[]{:S(2)}) copy-start(f32[3584]{0:T(1024)} %subtract_divide_fusion.84) | copy-start | bytes 43012
  1620.2 119.6 %copy-start.37 = (f32[3584]{0:T(1024)S(1)}, f32[3584]{0:T(1024)}, u32[]{:S(2)}) copy-start(f32[3584]{0:T(1024)} %get-tuple-element.438) | copy-start | bytes 43012
  1620.2 119.6 %copy-start.38 = (f32[3584]{0:T(1024)S(1)}, f32[3584]{0:T(1024)}, u32[]{:S(2)}) copy-start(f32[3584]{0:T(1024)} %get-tuple-element.439) | copy-start | bytes 43012
  1620.2 119.6 %copy-start.39 = (f32[3584]{0:T(1024)S(1)}, f32[3584]{0:T(1024)}, u32[]{:S(2)}) copy-start(f32[3584]{0:T(1024)} %get-tuple-element.441) | copy-start | bytes 43012
  1620.2 119.6 %copy-start.40 = (f32[3584]{0:T(1024)S(1)}, f32[3584]{0:T(1024)}, u32[]{:S(2)}) copy-start(f32[3584]{0:T(1024)} %get-tuple-element.467) | copy-start | bytes 43012
  1739.4 5.5 copy-start.47
  1739.4 5.5 copy-start.48
  1739.4 5.5 copy-start.49
  1739.4 5.5 copy-start.50
  1739.4 5.5 copy-start.51
  1739.4 5.5 copy-start.52
  1739.4 5.5 copy-start.53
Sparse Core Ops, SparseCore 0:
  326.4 133.6 all-reduce.2
where the time goes:
time: 1790 us; the launch traced here: 1760 us
  other arithmetic  1420 us (79%)
  blocking collectives  187 us (10%)
  local copies, waits for them, and re-layouts  116 us (6%)
    div x50, other arithmetic, cholesky_solve(): lower[i, j] = accum / pivot  892 us
    sqrt x8, other arithmetic, cholesky_solve(): pivot = jnp.sqrt(accum)  224 us
    div x2, other arithmetic, cholesky_solve(): value = accum / lower[i, i]  150 us
    div x5, other arithmetic, cholesky_solve(): result[i] = accum / lower[i, i]  127 us
    psum x1, blocking collectives, shards(): cross, gram = lax.psum((cross, gram), 'site')  122 us
    gather x1, local copies, waits for them, and re-layouts, prior_mean(): picked = jnp.take(window, local, axis=1)  98.9 us
    psum x1, blocking collectives, shards(): pull, lgram = lax.psum((pull, lgram_part), 'sp')  64.7 us
  transfers between devices with their start and end apart: 2, of which 0 were waited for; matrix products, arithmetic and copies ran while one was open for 70% of the time, Pallas kernels for 0%

commit v1 on v0

v1 whole, which is shorter than its diff:
```python
import functools

import jax
import jax.numpy as jnp
from jax import lax
from jax.experimental import pallas as pl
from jax.experimental.pallas import tpu as pltpu
from jax.sharding import PartitionSpec as P

F32 = jnp.float32
BF16 = jnp.bfloat16
MESH = pl.DeviceIdType.MESH

Z = 8
CORES = 2
K = 16
NBR = 15
CHUNK = 256
RIM = 1536
WINDOW = RIM + CHUNK
HALF = 8
STEP = 96

N_COEF = (0.7978845828848753, 0.561783412736638, 0.19921040380039692, 0.039025408597369395, 0.0036777514496204662)
D_COEF = (1.0, 1.1595221251207712, 0.6411219754723788, 0.20649649681102156, 0.03902744122918637, 0.003677727281734947)
inv_root_two_pi = 0.3989422804014327


def poly(coef, u):
    acc = u * coef[-1] + coef[-2]
    for a in coef[-3::-1]:
        acc = acc * u + a
    return acc


def split(x):
    hi = x.astype(BF16)
    return hi, (x - hi.astype(F32)).astype(BF16)


def dot(a, b, dims):
    return lax.dot_general(a, b, (dims, ((), ())), preferred_element_type=F32)


def blocks_sum(p, rows, cols):
    return (p[:rows, :cols] + p[:rows, cols:]) + (p[rows:, :cols] + p[rows:, cols:])


def cholesky(base, extra):
    width = extra[0].shape[1]
    row = lax.broadcasted_iota(jnp.int32, (HALF, width), 0)
    top, bot = [], []
    for k in range(K):
        diag = jnp.where(row == k % HALF, extra[k], 0.0)
        column = base[:, k : k + 1]
        if k < HALF:
            top.append(column[:HALF] + diag)
            bot.append(column[HALF:] + jnp.zeros_like(diag))
        else:
            top.append(None)
            bot.append(column[HALF:] + diag)
    scales = []
    for j in range(K):
        d = top[j][j : j + 1] if j < HALF else bot[j][j - HALF : j - HALF + 1]
        r = lax.rsqrt(d)
        scales.append(r)
        bot[j] = bot[j] * r
        if j < HALF:
            top[j] = top[j] * r
        for k in range(j + 1, K):
            if k < HALF:
                s = top[j][k : k + 1]
                top[k] = top[k] - top[j] * s
                bot[k] = bot[k] - bot[j] * s
            else:
                bot[k] = bot[k] - bot[j] * bot[j][k - HALF : k - HALF + 1]
    return top, bot, scales


def solve(factor, rhs, noise):
    top, bot, scales = factor
    rt, rb = rhs[:HALF], rhs[HALF:]
    middle = []
    for j in range(K):
        y = (rt[j : j + 1] if j < HALF else rb[j - HALF : j - HALF + 1]) * scales[j]
        if noise is not None:
            y = y + noise[j : j + 1]
        middle.append(y)
        if j < HALF:
            rt = rt - top[j] * y
        rb = rb - bot[j] * y
    row = lax.broadcasted_iota(jnp.int32, rt.shape, 0)
    xt, xb = jnp.zeros_like(rt), jnp.zeros_like(rt)
    for j in range(K - 1, -1, -1):
        terms = bot[j] * xb
        if j < HALF:
            terms = terms + top[j] * xt
        x = (middle[j] - jnp.sum(terms, axis=0, keepdims=True)) * scales[j]
        if j < HALF:
            xt = jnp.where(row == j, x, xt)
        else:
            xb = jnp.where(row == j - HALF, x, xb)
    return jnp.concatenate([xt, xb], axis=0)


def kernel(
    n_site,
    n_sp,
    presence,
    noise,
    factors,
    loadings,
    precision,
    neighbours,
    weights,
    variance,
    factor_noise,
    utilities,
    new_loadings,
    new_factors,
    fs,
    draws,
    window,
    onehot,
    gram_z,
    gram_x,
    cross_z,
    cross_x,
    lgram_mine,
    lgram_pair,
    lgram_y,
    pull_out,
    pull_pair,
    pull_mine,
    pull_y,
    rim_sems,
    gz_sems,
    gx_sems,
    cz_sems,
    cx_sems,
    lp_sems,
    ly_sems,
    pp_sems,
    py_sems,
    fy_sems,
    fp_sems,
):
    nx = n_site // Z
    ny = n_sp // CORES
    busy = ny - 1
    rows = factors.shape[1]
    species = loadings.shape[1]
    steps = rows // CHUNK

    site = lax.axis_index("site")
    sp = lax.axis_index("sp")
    x, z = site // Z, site % Z
    y, core = sp // CORES, sp % CORES
    pair = y * CORES + (1 - core)
    ahead = (site + 1) % n_site
    behind = (site + n_site - 1) % n_site

    def z_peer(d):
        return x * Z + (z + d) % Z

    def x_peer(d):
        return ((x + d) % nx) * Z + z

    barrier = pltpu.get_barrier_semaphore()
    greeted = [{"site": z_peer(d)} for d in range(1, Z)]
    greeted += [{"site": x_peer(d)} for d in range(1, nx)]
    greeted += [{"site": ahead}, {"site": behind}]
    greeted += [{"sp": ((y + d) % ny) * CORES + core} for d in range(1, ny)]
    greeted += [{"sp": pair}]
    for peer in greeted:
        pl.semaphore_signal(barrier, inc=1, device_id=peer, device_id_type=MESH)

    def remote(src, dst, sems, send, recv, peer):
        return pltpu.make_async_remote_copy(
            src_ref=src,
            dst_ref=dst,
            send_sem=sems.at[0, send],
            recv_sem=sems.at[1, recv],
            device_id=peer,
            device_id_type=MESH,
        )

    def spread_z(buf, sems):
        copies = []
        for d in range(1, Z):
            copy = remote(buf.at[z], buf.at[z], sems, d, d, {"site": z_peer(d)})
            copy.start()
            copies.append(copy)
        return copies

    def spread_x(buf, sems):
        copies = []
        for d in range(1, nx):
            copy = remote(buf.at[x], buf.at[x], sems, d, d, {"site": x_peer(d)})
            copy.start()
            copies.append(copy)
        return copies

    def gather_z(buf, sems):
        for d in range(1, Z):
            s = (z + Z - d) % Z
            remote(buf.at[s], buf.at[s], sems, d, d, {"site": z_peer(d)}).wait_recv()
        acc = buf[0]
        for s in range(1, Z):
            acc = acc + buf[s]
        return acc

    def gather_x(buf, sems):
        for d in range(1, nx):
            s = (x + nx - d) % nx
            remote(buf.at[s], buf.at[s], sems, d, d, {"site": x_peer(d)}).wait_recv()
        acc = buf[0]
        for s in range(1, nx):
            acc = acc + buf[s]
        return acc

    started = []

    f = factors[...]
    hi, lo = split(f)
    fs[0:16, :] = hi
    fs[16:32, :] = lo
    fs[32:48, :] = hi
    window[:, RIM:] = f
    l_hi, l_lo = split(loadings[...])
    ls = jnp.concatenate([l_hi, l_hi, l_lo], axis=0)

    both = jnp.concatenate([hi, lo], axis=0)
    products = dot(both, both, ((1,), (1,)))
    gram_part = blocks_sum(products, K, K)
    zeros = jnp.zeros((K, species), F32)
    gram_z[z] = zeros
    gram_z[z, :, 0:K] = gram_part

    pl.semaphore_wait(barrier, len(greeted))

    rim = remote(
        factors.at[:, rows - RIM : rows],
        window.at[:, 0:RIM],
        rim_sems,
        0,
        0,
        {"site": ahead},
    )
    started += spread_z(gram_z, gz_sems)
    rim.start()
    started.append(rim)

    def draw_step(i, acc):
        r0 = pl.multiple_of(i * CHUNK, CHUNK)
        mean = dot(fs[:, pl.ds(r0, CHUNK)], ls, ((0,), (0,)))
        there = presence[pl.ds(r0, CHUNK), :] > 0
        t = jnp.where(there, mean, -mean)
        u = jnp.abs(t)
        density = jnp.exp(-0.5 * t * t) * inv_root_two_pi
        num = poly(N_COEF, u)
        den = poly(D_COEF, u)
        full = u * den + num
        negative = t < 0.0
        v = jnp.where(negative, num, density * full) / jnp.where(negative, den, full - density * den)
        s = v + jnp.maximum(t, 0.0)
        spread = jnp.maximum(1.0 - v * (v + u), 0.0)
        draw = jnp.where(there, s, -s) + jnp.sqrt(spread) * noise[pl.ds(r0, CHUNK), :].astype(F32)
        d_hi, d_lo = split(draw)
        utilities[pl.ds(r0, CHUNK), :] = d_hi
        pieces = jnp.concatenate([d_hi, d_lo], axis=1)
        draws[pl.ds(r0, CHUNK), :] = pieces
        return acc + dot(fs[0:32, pl.ds(r0, CHUNK)], pieces, ((1,), (0,)))

    acc = jnp.zeros((2 * K, 2 * species), F32)
    acc = lax.fori_loop(0, steps // 2, draw_step, acc)
    gram_x[x] = gather_z(gram_z, gz_sems)
    started += spread_x(gram_x, gx_sems)
    acc = lax.fori_loop(steps // 2, steps, draw_step, acc)
    cross_z[z] = blocks_sum(acc, K, species)
    started += spread_z(cross_z, cz_sems)

    gram = gather_x(gram_x, gx_sems)[:, 0:K]
    factor = cholesky(gram, [precision[k : k + 1, :] for k in range(K)])
    cross_x[x] = gather_z(cross_z, cz_sems)
    started += spread_x(cross_x, cx_sems)

    chunk = jnp.minimum(sp, CORES * busy - 1)
    c0 = pl.multiple_of(chunk * CHUNK, CHUNK)
    base = site * rows + chunk * CHUNK - RIM
    onehot[...] = jnp.zeros_like(onehot)
    iota = lax.broadcasted_iota(jnp.int32, (224, 128), 0)

    def mark(k, carry):
        ids = neighbours[pl.ds(k, 1), pl.ds(c0, CHUNK)]
        w = jnp.where(ids >= 0, weights[pl.ds(k, 1), pl.ds(c0, CHUNK)], 0.0)
        for q in range(CHUNK // 128):
            first = pl.multiple_of(RIM - STEP + 128 * q - STEP * k, 32)
            lanes = slice(128 * q, 128 * (q + 1))
            hit = iota == ids[:, lanes] - (base + first)
            onehot[pl.ds(first, 224), lanes] += jnp.where(hit, w[:, lanes], 0.0)
        return carry

    lax.fori_loop(0, NBR, mark, 0)
    rim.wait_recv()

    def gather_step(b, acc):
        r0 = pl.multiple_of(b * 256, 256)
        m_hi, m_lo = split(onehot[pl.ds(r0, 256), :])
        w_hi, w_lo = split(window[:, pl.ds(pl.multiple_of(c0 + r0, 256), 256)])
        return acc + dot(
            jnp.concatenate([w_hi, w_lo], axis=0),
            jnp.concatenate([m_hi, m_lo], axis=1),
            ((1,), (0,)),
        )

    prior = lax.fori_loop(0, WINDOW // 256, gather_step, jnp.zeros((2 * K, 2 * CHUNK), F32))
    prior = blocks_sum(prior, K, CHUNK)
    inverse = 1.0 / variance[:, pl.ds(c0, CHUNK)]
    shift = prior * inverse

    cross = gather_x(cross_x, cx_sems)
    fresh = solve(factor, cross, None)
    new_loadings[...] = fresh

    n_hi, n_lo = split(fresh)
    narrow = jnp.concatenate([n_hi, n_lo], axis=0)
    lgram_part = blocks_sum(dot(narrow, narrow, ((1,), (1,))), K, K)
    lgram_mine[...] = zeros
    lgram_mine[:, 0:K] = lgram_part
    copy = remote(lgram_mine, lgram_pair, lp_sems, 0, 0, {"sp": pair})
    copy.start()
    started.append(copy)

    zero = jnp.zeros_like(n_hi)
    wide = jnp.concatenate(
        [jnp.concatenate([n_hi, n_hi], axis=1), jnp.concatenate([n_lo, zero], axis=1)],
        axis=0,
    )

    def pull_of(t, c):
        r0 = pl.multiple_of((t * CORES + c) * CHUNK, CHUNK)
        p = dot(wide, draws[pl.ds(r0, CHUNK), :], ((1,), (1,)))
        return p[:K] + p[K:]

    for e in range(1, busy + 1):
        t = (y + e) % busy
        pull_out[e - 1] = pull_of(t, 1 - core)
        copy = remote(pull_out.at[e - 1], pull_pair.at[e - 1], pp_sems, e - 1, e - 1, {"sp": pair})
        copy.start()
        started.append(copy)

    remote(lgram_mine, lgram_pair, lp_sems, 0, 0, {"sp": pair}).wait_recv()
    lgram_y[y] = lgram_mine[...] + lgram_pair[...]
    for d in range(1, ny):
        peer = {"sp": ((y + d) % ny) * CORES + core}
        copy = remote(lgram_y.at[y], lgram_y.at[y], ly_sems, d, d, peer)
        copy.start()
        started.append(copy)

    for e in range(1, busy + 1):
        t = (y + e) % busy
        mine = pull_of(t, core)
        remote(pull_out.at[e - 1], pull_pair.at[e - 1], pp_sems, e - 1, e - 1, {"sp": pair}).wait_recv()
        pull_mine[e - 1] = mine + pull_pair[e - 1]
        copy = remote(pull_mine.at[e - 1], pull_y.at[y], py_sems, e, y, {"sp": t * CORES + core})
        if e < busy:
            copy.start()
            started.append(copy)
        else:

            @pl.when(y == busy)
            def _():
                copy.start()

            last_pull = copy

    for d in range(1, ny):
        s = (y + ny - d) % ny
        peer = {"sp": ((y + d) % ny) * CORES + core}
        remote(lgram_y.at[s], lgram_y.at[s], ly_sems, d, d, peer).wait_recv()

    def factors_to(sems, send, recv, index, peer):
        lanes = pl.ds(pl.multiple_of(index * CHUNK, CHUNK), CHUNK)
        return remote(new_factors.at[:, lanes], new_factors.at[:, lanes], sems, send, recv, peer)

    @pl.when(y < busy)
    def _():
        lgram = lgram_y[0]
        for s in range(1, ny):
            lgram = lgram + lgram_y[s]
        site_factor = cholesky(lgram[:, 0:K], [inverse] * K)
        total = pull_mine[busy - 1] + shift
        for d in range(1, ny):
            s = (y + d) % ny
            remote(pull_y.at[s], pull_y.at[s], py_sems, 0, s, {"sp": s * CORES + core}).wait_recv()
            total = total + pull_y[s]
        result = solve(site_factor, total, factor_noise[:, pl.ds(c0, CHUNK)])
        new_factors[:, pl.ds(c0, CHUNK)] = result
        for d in range(1, ny):
            t = (y + d) % ny
            factors_to(fy_sems, d, y, y * CORES + core, {"sp": t * CORES + core}).start()
        factors_to(fp_sems, y, y, y * CORES + core, {"sp": pair}).start()

    for e in range(1, busy + 1):
        s = (y + busy - e) % busy

        def hand_on():
            factors_to(fy_sems, 0, s, s * CORES + core, {"sp": s * CORES + core}).wait_recv()
            factors_to(fp_sems, s, s, s * CORES + core, {"sp": pair}).start()

        if e < busy:
            hand_on()
        else:
            pl.when(y == busy)(hand_on)

    for s in range(busy):
        factors_to(fp_sems, s, s, s * CORES + (1 - core), {"sp": pair}).wait_recv()

    for copy in started:
        copy.wait_send()
    for s in range(busy):
        factors_to(fp_sems, s, s, s * CORES + core, {"sp": pair}).wait_send()

    @pl.when(y == busy)
    def _():
        last_pull.wait_send()

    @pl.when(y < busy)
    def _():
        for d in range(1, ny):
            t = (y + d) % ny
            factors_to(fy_sems, d, y, y * CORES + core, {"sp": t * CORES + core}).wait_send()


def solution(mesh):
    n_site, n_sp = mesh.shape["site"], mesh.shape["sp"]
    nx, ny = n_site // Z, n_sp // CORES
    busy = ny - 1

    def shards(presence, noise, factors, loadings, precision, neighbours, weights, variance, factor_noise):
        rows, species = presence.shape
        assert rows == busy * CORES * CHUNK and species == 128
        vmem = pl.BlockSpec(memory_space=pltpu.VMEM)
        sems = pltpu.SemaphoreType.DMA
        return pl.pallas_call(
            functools.partial(kernel, n_site, n_sp),
            out_shape=(
                jax.ShapeDtypeStruct((rows, species), BF16),
                jax.ShapeDtypeStruct((K, species), F32),
                jax.ShapeDtypeStruct((K, rows), F32),
            ),
            in_specs=[vmem] * 9,
            out_specs=(vmem,) * 3,
            scratch_shapes=[
                pltpu.VMEM((3 * K, rows), BF16),
                pltpu.VMEM((rows, 2 * species), BF16),
                pltpu.VMEM((K, RIM + rows), F32),
                pltpu.VMEM((WINDOW, CHUNK), F32),
                pltpu.VMEM((Z, K, species), F32),
                pltpu.VMEM((nx, K, species), F32),
                pltpu.VMEM((Z, K, species), F32),
                pltpu.VMEM((nx, K, species), F32),
                pltpu.VMEM((K, species), F32),
                pltpu.VMEM((K, species), F32),
                pltpu.VMEM((ny, K, species), F32),
                pltpu.VMEM((busy, K, CHUNK), F32),
                pltpu.VMEM((busy, K, CHUNK), F32),
                pltpu.VMEM((busy, K, CHUNK), F32),
                pltpu.VMEM((ny, K, CHUNK), F32),
                sems((2, 1)),
                sems((2, Z)),
                sems((2, nx)),
                sems((2, Z)),
                sems((2, nx)),
                sems((2, 1)),
                sems((2, ny)),
                sems((2, busy)),
                sems((2, ny)),
                sems((2, ny)),
                sems((2, busy)),
            ],
            compiler_params=pltpu.CompilerParams(
                collective_id=0,
                has_side_effects=True,
                vmem_limit_bytes=40 * 1024 * 1024,
            ),
        )(presence, noise, factors, loadings, precision, neighbours, weights, variance.reshape(1, rows), factor_noise)

    in_specs = (
        P("site", "sp"),
        P("site", "sp"),
        P(None, "site"),
        P(None, "sp"),
        P(None, "sp"),
        P(None, "site"),
        P(None, "site"),
        P("site"),
        P(None, "site"),
    )
    out_specs = (P("site", "sp"), P(None, "sp"), P(None, "site"))
    return jax.shard_map(shards, mesh=mesh, in_specs=in_specs, out_specs=out_specs, check_vma=False)
```

time: 1790 us -> 62.4 us (0.03); the launches traced: 1760 us -> 62 us
  other arithmetic: 1420 us -> 0 us
  blocking collectives: 187 us -> 0 us
  local copies, waits for them, and re-layouts: 116 us -> 10.8 us
  Pallas kernels: 0 us -> 50.6 us
    div x57 -> x0, other arithmetic: 1170 us -> none  [the longest x50 892 us: cholesky_solve(): lower[i, j] = accum / pivot]
    sqrt x8 -> x0, other arithmetic: 224 us -> none  [cholesky_solve(): pivot = jnp.sqrt(accum)]
    psum x2 -> x0, blocking collectives: 187 us -> none  [the longest x1 122 us: shards(): cross, gram = lax.psum((cross, gram), 'site')]
    gather x1 -> x0, local copies, waits for them, and re-layouts: 98.9 us -> none  [prior_mean(): picked = jnp.take(window, local, axis=1)]
    pallas_call x0 -> x1, Pallas kernels: none -> 50.6 us  [shards(): pl.pallas_call(functools.partial(kernel, n_site, n_sp), out_shape=(jax.Sh...]
    reduce_sum x1 -> x0, other arithmetic: 21.2 us -> none  [prior_mean(): return jnp.sum(picked * scaled[None, :, :], axis=1)]
  transfers between devices with their start and end apart: 2 -> 0, of which waited for: 0 -> 0; matrix products, arithmetic and copies ran while one was open for 70% -> 0% of each run, Pallas kernels for 0% -> 0%
where the time goes in v1:
time: 62.4 us; the launch traced here: 62 us
  Pallas kernels  50.6 us (81%)
  local copies, waits for them, and re-layouts  10.8 us (17%)
  between operations  0.66 us (1%)
    pallas_call x1, Pallas kernels, shards(): pl.pallas_call(functools.partial(kernel, n_site, n_sp), out_shape=(jax.Sh...  50.6 us
    unnamed x19, local copies, waits for them, and re-layouts  10 us

profile of v1, /device:TPU:1, one launch (start us, length us, event | category | flops | bytes accessed | tf_op | source)
XLA Modules:
  0.0 62.0 jit_solution(5528623708730766966)
XLA Ops:
  0.6 0.7 %reshape.9.variance = f32[1,3584]{1,0:T(1,128)S(1)} reshape(f32[3584]{0:T(1024)} %param.16) | data formatting | bytes 28672 | tf_op jit(solution)/shard_map/reshape | solution.py:488
  1.4 0.0 copy-start
  1.4 1.5 %copy-done = s32[3584,128]{1,0:T(8,128)S(1)} copy-done((s32[3584,128]{1,0:T(8,128)S(1)}, s32[3584,128]{1,0:T(8,128)}, u32[]{:S(2)}) %copy-start) | copy-done | bytes 1835032
  2.9 0.0 copy-start.1
  2.9 1.2 %copy-done.1 = bf16[3584,128]{1,0:T(8,128)(2,1)S(1)} copy-done((bf16[3584,128]{1,0:T(8,128)(2,1)S(1)}, bf16[3584,128]{1,0:T(8,128)(2,1)}, u32[]{:S(2)}) %copy-start.1) | copy-done | bytes 917528
  4.0 0.0 copy-start.2
  4.0 0.9 %copy-done.2 = f32[16,3584]{1,0:T(8,128)S(1)} copy-done((f32[16,3584]{1,0:T(8,128)S(1)}, f32[16,3584]{1,0:T(8,128)}, u32[]{:S(2)}) %copy-start.2) | copy-done | bytes 229400
  5.0 0.0 copy-start.3
  5.0 0.9 %copy-done.3 = s32[15,3584]{1,0:T(8,128)S(1)} copy-done((s32[15,3584]{1,0:T(8,128)S(1)}, s32[15,3584]{1,0:T(8,128)}, u32[]{:S(2)}) %copy-start.3) | copy-done | bytes 215064
  5.9 0.0 copy-start.4
  5.9 0.9 %copy-done.4 = f32[15,3584]{1,0:T(8,128)S(1)} copy-done((f32[15,3584]{1,0:T(8,128)S(1)}, f32[15,3584]{1,0:T(8,128)}, u32[]{:S(2)}) %copy-start.4) | copy-done | bytes 215064
  6.9 0.0 copy-start.5
  6.9 0.9 %copy-done.5 = f32[16,3584]{1,0:T(8,128)S(1)} copy-done((f32[16,3584]{1,0:T(8,128)S(1)}, f32[16,3584]{1,0:T(8,128)}, u32[]{:S(2)}) %copy-start.5) | copy-done | bytes 229400
  7.8 0.0 copy-start.6
  7.8 0.7 %copy-done.6 = f32[16,128]{1,0:T(8,128)S(1)} copy-done((f32[16,128]{1,0:T(8,128)S(1)}, f32[16,128]{1,0:T(8,128)}, u32[]{:S(2)}) %copy-start.6) | copy-done | bytes 8216
  8.5 0.0 copy-start.7
  8.5 0.7 %copy-done.7 = f32[16,128]{1,0:T(8,128)S(1)} copy-done((f32[16,128]{1,0:T(8,128)S(1)}, f32[16,128]{1,0:T(8,128)}, u32[]{:S(2)}) %copy-start.7) | copy-done | bytes 8216
  9.2 50.6 %shard_map.112 = (bf16[3584,128]{1,0:T(8,128)(2,1)S(1)}, f32[16,128]{1,0:T(8,128)S(1)}, f32[16,3584]{1,0:T(8,128)S(1)}) custom-call(s32[3584,128]{1,0:T(8,128)S(1)} %copy-done, bf16[3584,128]{1,0:T(8,128)(2,1)S(1)} %copy-done.1, f32[16,3584]{1,0:T(8,128)S(1)} %copy-done.2, f32[16,128]{1,0:T(8,128)S(1)} %copy-done.6, f32[16,128]{1,0:T(8,128)S(1)} %copy-done.7, ...), custom_call_target="tpu_custom_call" | custom-call | tf_op jit(solution)/shard_map/pallas_call | solution.py:446
  59.8 0.9 %copy.15 = bf16[3584,128]{1,0:T(8,128)(2,1)} copy(bf16[3584,128]{1,0:T(8,128)(2,1)S(1)} %get-tuple-element.6) | data formatting | bytes 1835008
  60.7 0.6 copy.16
  61.3 0.7 %copy.17 = f32[16,3584]{1,0:T(8,128)} copy(f32[16,3584]{1,0:T(8,128)S(1)} %get-tuple-element.8) | data formatting | bytes 458752
Async XLA Ops:
  1.4 1.5 %copy-start = (s32[3584,128]{1,0:T(8,128)S(1)}, s32[3584,128]{1,0:T(8,128)}, u32[]{:S(2)}) copy-start(s32[3584,128]{1,0:T(8,128)} %presence.1) | copy-start | bytes 5505028
  2.9 1.2 %copy-start.1 = (bf16[3584,128]{1,0:T(8,128)(2,1)S(1)}, bf16[3584,128]{1,0:T(8,128)(2,1)}, u32[]{:S(2)}) copy-start(bf16[3584,128]{1,0:T(8,128)(2,1)} %noise.1) | copy-start | bytes 2752516
  4.0 0.9 %copy-start.2 = (f32[16,3584]{1,0:T(8,128)S(1)}, f32[16,3584]{1,0:T(8,128)}, u32[]{:S(2)}) copy-start(f32[16,3584]{1,0:T(8,128)} %factors.1) | copy-start | bytes 688132
  5.0 0.9 %copy-start.3 = (s32[15,3584]{1,0:T(8,128)S(1)}, s32[15,3584]{1,0:T(8,128)}, u32[]{:S(2)}) copy-start(s32[15,3584]{1,0:T(8,128)} %neighbours.1) | copy-start | bytes 645124
  5.9 0.9 %copy-start.4 = (f32[15,3584]{1,0:T(8,128)S(1)}, f32[15,3584]{1,0:T(8,128)}, u32[]{:S(2)}) copy-start(f32[15,3584]{1,0:T(8,128)} %weights.1) | copy-start | bytes 645124
  6.9 0.9 %copy-start.5 = (f32[16,3584]{1,0:T(8,128)S(1)}, f32[16,3584]{1,0:T(8,128)}, u32[]{:S(2)}) copy-start(f32[16,3584]{1,0:T(8,128)} %factor_noise.1) | copy-start | bytes 688132
  7.8 0.7 %copy-start.6 = (f32[16,128]{1,0:T(8,128)S(1)}, f32[16,128]{1,0:T(8,128)}, u32[]{:S(2)}) copy-start(f32[16,128]{1,0:T(8,128)} %loadings.1) | copy-start | bytes 24580
  8.5 0.7 %copy-start.7 = (f32[16,128]{1,0:T(8,128)S(1)}, f32[16,128]{1,0:T(8,128)}, u32[]{:S(2)}) copy-start(f32[16,128]{1,0:T(8,128)} %precision.1) | copy-start | bytes 24580

commit v2 on v1

--- a/solution.py
+++ b/solution.py
@@ -103,9 +103,29 @@
     return jnp.concatenate([xt, xb], axis=0)
 
 
+def far_first(n):
+    return sorted(range(1, n), key=lambda d: -min(d, n - d))
+
+
 def kernel(
     n_site,
     n_sp,
+    presence_hbm,
+    noise_hbm,
+    factors_hbm,
+    loadings_hbm,
+    precision_hbm,
+    neighbours_hbm,
+    weights_hbm,
+    variance_hbm,
+    factor_noise_hbm,
+    utilities_hbm,
+    new_loadings_hbm,
+    new_factors_hbm,
+    utilities,
+    new_loadings,
+    new_factors,
+    out_sems,
     presence,
     noise,
     factors,
@@ -115,9 +135,7 @@
     weights,
     variance,
     factor_noise,
-    utilities,
-    new_loadings,
-    new_factors,
+    in_sems,
     fs,
     draws,
     window,
@@ -149,8 +167,9 @@
     ny = n_sp // CORES
     busy = ny - 1
     rows = factors.shape[1]
+    steps = rows // CHUNK
+    cuts = (0, min(2, steps // 2) * CHUNK, steps // 2 * CHUNK, rows)
     species = loadings.shape[1]
-    steps = rows // CHUNK
 
     site = lax.axis_index("site")
     sp = lax.axis_index("sp")
@@ -187,7 +206,7 @@
 
     def spread_z(buf, sems):
         copies = []
-        for d in range(1, Z):
+        for d in far_first(Z):
             copy = remote(buf.at[z], buf.at[z], sems, d, d, {"site": z_peer(d)})
             copy.start()
             copies.append(copy)
@@ -195,7 +214,7 @@
 
     def spread_x(buf, sems):
         copies = []
-        for d in range(1, nx):
+        for d in far_first(nx):
             copy = remote(buf.at[x], buf.at[x], sems, d, d, {"site": x_peer(d)})
             copy.start()
             copies.append(copy)
@@ -219,8 +238,27 @@
             acc = acc + buf[s]
         return acc
 
+    chunk = jnp.minimum(sp, CORES * busy - 1)
+    c0 = pl.multiple_of(chunk * CHUNK, CHUNK)
+    mine = pl.ds(c0, CHUNK)
+    loads = [(factors_hbm, factors), (loadings_hbm, loadings)]
+    for a, b in zip(cuts, cuts[1:]):
+        loads.append((presence_hbm.at[a:b], presence.at[a:b]))
+        loads.append((noise_hbm.at[a:b], noise.at[a:b]))
+    loads += [
+        (neighbours_hbm.at[:, mine], neighbours),
+        (weights_hbm.at[:, mine], weights),
+        (precision_hbm, precision),
+        (variance_hbm.at[:, mine], variance),
+        (factor_noise_hbm.at[:, mine], factor_noise),
+    ]
+    loads = [pltpu.make_async_copy(a, b, in_sems.at[i]) for i, (a, b) in enumerate(loads)]
+    for load in loads:
+        load.start()
     started = []
 
+    loads[0].wait()
+    loads[1].wait()
     f = factors[...]
     hi, lo = split(f)
     fs[0:16, :] = hi
@@ -236,20 +274,6 @@
     zeros = jnp.zeros((K, species), F32)
     gram_z[z] = zeros
     gram_z[z, :, 0:K] = gram_part
-
-    pl.semaphore_wait(barrier, len(greeted))
-
-    rim = remote(
-        factors.at[:, rows - RIM : rows],
-        window.at[:, 0:RIM],
-        rim_sems,
-        0,
-        0,
-        {"site": ahead},
-    )
-    started += spread_z(gram_z, gz_sems)
-    rim.start()
-    started.append(rim)
 
     def draw_step(i, acc):
         r0 = pl.multiple_of(i * CHUNK, CHUNK)
@@ -273,27 +297,44 @@
         return acc + dot(fs[0:32, pl.ds(r0, CHUNK)], pieces, ((1,), (0,)))
 
     acc = jnp.zeros((2 * K, 2 * species), F32)
-    acc = lax.fori_loop(0, steps // 2, draw_step, acc)
+    for piece in range(2):
+        loads[2 + 2 * piece].wait()
+        loads[3 + 2 * piece].wait()
+        acc = lax.fori_loop(cuts[piece] // CHUNK, cuts[piece + 1] // CHUNK, draw_step, acc)
+
+    pl.semaphore_wait(barrier, len(greeted))
+
+    rim = remote(
+        factors.at[:, rows - RIM : rows],
+        window.at[:, 0:RIM],
+        rim_sems,
+        0,
+        0,
+        {"site": ahead},
+    )
+    started += spread_z(gram_z, gz_sems)
+    rim.start()
+    started.append(rim)
+
+    loads[6].wait()
+    loads[7].wait()
+    acc = lax.fori_loop(cuts[2] // CHUNK, steps, draw_step, acc)
+    cross_z[z] = blocks_sum(acc, K, species)
+    started += spread_z(cross_z, cz_sems)
+    stores = [pltpu.make_async_copy(utilities, utilities_hbm, out_sems.at[0])]
+    stores[0].start()
     gram_x[x] = gather_z(gram_z, gz_sems)
     started += spread_x(gram_x, gx_sems)
-    acc = lax.fori_loop(steps // 2, steps, draw_step, acc)
-    cross_z[z] = blocks_sum(acc, K, species)
-    started += spread_z(cross_z, cz_sems)
-
-    gram = gather_x(gram_x, gx_sems)[:, 0:K]
-    factor = cholesky(gram, [precision[k : k + 1, :] for k in range(K)])
-    cross_x[x] = gather_z(cross_z, cz_sems)
-    started += spread_x(cross_x, cx_sems)
-
-    chunk = jnp.minimum(sp, CORES * busy - 1)
-    c0 = pl.multiple_of(chunk * CHUNK, CHUNK)
+
+    for load in loads[8:]:
+        load.wait()
     base = site * rows + chunk * CHUNK - RIM
     onehot[...] = jnp.zeros_like(onehot)
     iota = lax.broadcasted_iota(jnp.int32, (224, 128), 0)
 
     def mark(k, carry):
-        ids = neighbours[pl.ds(k, 1), pl.ds(c0, CHUNK)]
-        w = jnp.where(ids >= 0, weights[pl.ds(k, 1), pl.ds(c0, CHUNK)], 0.0)
+        ids = neighbours[pl.ds(k, 1), :]
+        w = jnp.where(ids >= 0, weights[pl.ds(k, 1), :], 0.0)
         for q in range(CHUNK // 128):
             first = pl.multiple_of(RIM - STEP + 128 * q - STEP * k, 32)
             lanes = slice(128 * q, 128 * (q + 1))
@@ -316,12 +357,20 @@
 
     prior = lax.fori_loop(0, WINDOW // 256, gather_step, jnp.zeros((2 * K, 2 * CHUNK), F32))
     prior = blocks_sum(prior, K, CHUNK)
-    inverse = 1.0 / variance[:, pl.ds(c0, CHUNK)]
+    inverse = 1.0 / variance[...]
     shift = prior * inverse
+
+    cross_x[x] = gather_z(cross_z, cz_sems)
+    started += spread_x(cross_x, cx_sems)
+
+    gram = gather_x(gram_x, gx_sems)[:, 0:K]
+    factor = cholesky(gram, [precision[k : k + 1, :] for k in range(K)])
 
     cross = gather_x(cross_x, cx_sems)
     fresh = solve(factor, cross, None)
     new_loadings[...] = fresh
+    stores.append(pltpu.make_async_copy(new_loadings, new_loadings_hbm, out_sems.at[1]))
+    stores[1].start()
 
     n_hi, n_lo = split(fresh)
     narrow = jnp.concatenate([n_hi, n_lo], axis=0)
@@ -343,7 +392,10 @@
         p = dot(wide, draws[pl.ds(r0, CHUNK), :], ((1,), (1,)))
         return p[:K] + p[K:]
 
-    for e in range(1, busy + 1):
+    order = far_first(ny)
+    order.remove(busy)
+    order.append(busy)
+    for e in order:
         t = (y + e) % busy
         pull_out[e - 1] = pull_of(t, 1 - core)
         copy = remote(pull_out.at[e - 1], pull_pair.at[e - 1], pp_sems, e - 1, e - 1, {"sp": pair})
@@ -352,17 +404,17 @@
 
     remote(lgram_mine, lgram_pair, lp_sems, 0, 0, {"sp": pair}).wait_recv()
     lgram_y[y] = lgram_mine[...] + lgram_pair[...]
-    for d in range(1, ny):
+    for d in far_first(ny):
         peer = {"sp": ((y + d) % ny) * CORES + core}
         copy = remote(lgram_y.at[y], lgram_y.at[y], ly_sems, d, d, peer)
         copy.start()
         started.append(copy)
 
-    for e in range(1, busy + 1):
+    for e in order:
         t = (y + e) % busy
-        mine = pull_of(t, core)
+        part = pull_of(t, core)
         remote(pull_out.at[e - 1], pull_pair.at[e - 1], pp_sems, e - 1, e - 1, {"sp": pair}).wait_recv()
-        pull_mine[e - 1] = mine + pull_pair[e - 1]
+        pull_mine[e - 1] = part + pull_pair[e - 1]
         copy = remote(pull_mine.at[e - 1], pull_y.at[y], py_sems, e, y, {"sp": t * CORES + core})
         if e < busy:
             copy.start()
@@ -395,14 +447,14 @@
             s = (y + d) % ny
             remote(pull_y.at[s], pull_y.at[s], py_sems, 0, s, {"sp": s * CORES + core}).wait_recv()
             total = total + pull_y[s]
-        result = solve(site_factor, total, factor_noise[:, pl.ds(c0, CHUNK)])
+        result = solve(site_factor, total, factor_noise[...])
         new_factors[:, pl.ds(c0, CHUNK)] = result
-        for d in range(1, ny):
+        for d in far_first(ny):
             t = (y + d) % ny
             factors_to(fy_sems, d, y, y * CORES + core, {"sp": t * CORES + core}).start()
         factors_to(fp_sems, y, y, y * CORES + core, {"sp": pair}).start()
 
-    for e in range(1, busy + 1):
+    for e in order[busy - 2 :: -1] + [busy]:
         s = (y + busy - e) % busy
 
         def hand_on():
@@ -416,6 +468,9 @@
 
     for s in range(busy):
         factors_to(fp_sems, s, s, s * CORES + (1 - core), {"sp": pair}).wait_recv()
+
+    stores.append(pltpu.make_async_copy(new_factors, new_factors_hbm, out_sems.at[2]))
+    stores[2].start()
 
     for copy in started:
         copy.wait_send()
@@ -432,6 +487,20 @@
             t = (y + d) % ny
             factors_to(fy_sems, d, y, y * CORES + core, {"sp": t * CORES + core}).wait_send()
 
+    for store in stores:
+        store.wait()
+
+
+def write_out(a, b, c, a_out, b_out, c_out, sems):
+    cut = a.shape[0] // 4
+    pairs = [(a.at[i * cut : (i + 1) * cut], a_out.at[i * cut : (i + 1) * cut]) for i in range(4)]
+    pairs += [(b, b_out), (c, c_out)]
+    copies = [pltpu.make_async_copy(src, dst, sems.at[i]) for i, (src, dst) in enumerate(pairs)]
+    for copy in copies:
+        copy.start()
+    for copy in copies:
+        copy.wait()
+
 
 def solution(mesh):
     n_site, n_sp = mesh.shape["site"], mesh.shape["sp"]
@@ -441,18 +510,33 @@
     def shards(presence, noise, factors, loadings, precision, neighbours, weights, variance, factor_noise):
         rows, species = presence.shape
         assert rows == busy * CORES * CHUNK and species == 128
-        vmem = pl.BlockSpec(memory_space=pltpu.VMEM)
+        hbm = pl.BlockSpec(memory_space=pltpu.HBM)
         sems = pltpu.SemaphoreType.DMA
-        return pl.pallas_call(
+        out_shape = (
+            jax.ShapeDtypeStruct((rows, species), BF16),
+            jax.ShapeDtypeStruct((K, species), F32),
+            jax.ShapeDtypeStruct((K, rows), F32),
+        )
+        results = pl.pallas_call(
             functools.partial(kernel, n_site, n_sp),
-            out_shape=(
-                jax.ShapeDtypeStruct((rows, species), BF16),
-                jax.ShapeDtypeStruct((K, species), F32),
-                jax.ShapeDtypeStruct((K, rows), F32),
-            ),
-            in_specs=[vmem] * 9,
-            out_specs=(vmem,) * 3,
+            out_shape=out_shape,
+            in_specs=[hbm] * 9,
+            out_specs=(hbm,) * 3,
             scratch_shapes=[
+                pltpu.VMEM((rows, species), BF16),
+                pltpu.VMEM((K, species), F32),
+                pltpu.VMEM((K, rows), F32),
+                sems((3,)),
+                pltpu.VMEM((rows, species), jnp.int32),
+                pltpu.VMEM((rows, species), BF16),
+                pltpu.VMEM((K, rows), F32),
+                pltpu.VMEM((K, species), F32),
+                pltpu.VMEM((K, species), F32),
+                pltpu.VMEM((NBR, CHUNK), jnp.int32),
+                pltpu.VMEM((NBR, CHUNK), F32),
+                pltpu.VMEM((1, CHUNK), F32),
+                pltpu.VMEM((K, CHUNK), F32),
+                sems((13,)),
                 pltpu.VMEM((3 * K, rows), BF16),
                 pltpu.VMEM((rows, 2 * species), BF16),
                 pltpu.VMEM((K, RIM + rows), F32),
@@ -483,9 +567,16 @@
             compiler_params=pltpu.CompilerParams(
                 collective_id=0,
                 has_side_effects=True,
-                vmem_limit_bytes=40 * 1024 * 1024,
+                vmem_limit_bytes=60 * 1024 * 1024,
             ),
         )(presence, noise, factors, loadings, precision, neighbours, weights, variance.reshape(1, rows), factor_noise)
+        return pl.pallas_call(
+            write_out,
+            out_shape=out_shape,
+            in_specs=[hbm] * 3,
+            out_specs=(hbm,) * 3,
+            scratch_shapes=[sems((6,))],
+        )(*results)
 
     in_specs = (
         P("site", "sp"),

time: 62.4 us -> 84.4 us (1.35)
  Pallas kernels: 50.6 us -> 82.3 us
  local copies, waits for them, and re-layouts: 10.8 us -> 1.33 us
    pallas_call x1 -> x2, Pallas kernels: 50.6 us -> 82.3 us  [the longest x1 46.1 us: shards(): pl.pallas_call(functools.partial(kernel, n_site, n_sp), out_shape=out_sha...]
    unnamed x19 -> x0, local copies, waits for them, and re-layouts: 10 us -> none
where the time goes in v2:
time: 84.4 us; the launch traced here: 84.3 us
  Pallas kernels  82.3 us (98%)
  local copies, waits for them, and re-layouts  1.33 us (2%)
    pallas_call x1, Pallas kernels, shards(): pl.pallas_call(functools.partial(kernel, n_site, n_sp), out_shape=out_sha...  46.1 us
    pallas_call x1, Pallas kernels, shards(): pl.pallas_call(write_out, out_shape=out_shape, in_specs=[hbm] * 3, out_sp...  36.1 us

profile of v2, /device:TPU:1, one launch (start us, length us, event | category | flops | bytes accessed | tf_op | source)
XLA Modules:
  0.0 84.3 jit_solution(1389297788947710485)
XLA Ops:
  0.6 1.3 %reshape.9.variance_hbm = f32[1,3584]{1,0:T(1,128)} reshape(f32[3584]{0:T(1024)} %param.16) | data formatting | bytes 28672 | tf_op jit(solution)/shard_map/reshape | solution.py:572
  2.0 46.1 %shard_map.112 = (bf16[3584,128]{1,0:T(8,128)(2,1)}, f32[16,128]{1,0:T(8,128)}, f32[16,3584]{1,0:T(8,128)}) custom-call(s32[3584,128]{1,0:T(8,128)} %presence_hbm.1, bf16[3584,128]{1,0:T(8,128)(2,1)} %noise_hbm.1, f32[16,3584]{1,0:T(8,128)} %factors_hbm.1, f32[16,128]{1,0:T(8,128)} %loadings_hbm.1, f32[16,128]{1,0:T(8,128)} %precision_hbm.1, ...), custom_call_target="tpu_custom_call" | custom-call | tf_op jit(solution)/shard_map/pallas_call | solution.py:520
  48.1 36.1 %shard_map.113 = (bf16[3584,128]{1,0:T(8,128)(2,1)}, f32[16,128]{1,0:T(8,128)}, f32[16,3584]{1,0:T(8,128)}) custom-call(bf16[3584,128]{1,0:T(8,128)(2,1)} %get-tuple-element.6.a, f32[16,128]{1,0:T(8,128)} %get-tuple-element.7.b, f32[16,3584]{1,0:T(8,128)} %get-tuple-element.8.c), custom_call_target="tpu_custom_call" | custom-call | tf_op jit(solution)/shard_map/pallas_call | solution.py:573

commit v3 on v2

--- a/solution.py
+++ b/solution.py
@@ -20,6 +20,7 @@
 WINDOW = RIM + CHUNK
 HALF = 8
 STEP = 96
+PIECES = 4
 
 N_COEF = (0.7978845828848753, 0.561783412736638, 0.19921040380039692, 0.039025408597369395, 0.0036777514496204662)
 D_COEF = (1.0, 1.1595221251207712, 0.6411219754723788, 0.20649649681102156, 0.03902744122918637, 0.003677727281734947)
@@ -249,7 +250,7 @@
         (neighbours_hbm.at[:, mine], neighbours),
         (weights_hbm.at[:, mine], weights),
         (precision_hbm, precision),
-        (variance_hbm.at[:, mine], variance),
+        (variance_hbm, variance),
         (factor_noise_hbm.at[:, mine], factor_noise),
     ]
     loads = [pltpu.make_async_copy(a, b, in_sems.at[i]) for i, (a, b) in enumerate(loads)]
@@ -357,7 +358,7 @@
 
     prior = lax.fori_loop(0, WINDOW // 256, gather_step, jnp.zeros((2 * K, 2 * CHUNK), F32))
     prior = blocks_sum(prior, K, CHUNK)
-    inverse = 1.0 / variance[...]
+    inverse = 1.0 / variance[pl.ds(c0, CHUNK)].reshape(1, CHUNK)
     shift = prior * inverse
 
     cross_x[x] = gather_z(cross_z, cz_sems)
@@ -491,15 +492,20 @@
         store.wait()
 
 
-def write_out(a, b, c, a_out, b_out, c_out, sems):
-    cut = a.shape[0] // 4
-    pairs = [(a.at[i * cut : (i + 1) * cut], a_out.at[i * cut : (i + 1) * cut]) for i in range(4)]
-    pairs += [(b, b_out), (c, c_out)]
-    copies = [pltpu.make_async_copy(src, dst, sems.at[i]) for i, (src, dst) in enumerate(pairs)]
-    for copy in copies:
-        copy.start()
-    for copy in copies:
-        copy.wait()
+def write_out(a, b, c, a_out, b_out, c_out, a_mid, b_mid, c_mid, sems):
+    cut = a.shape[0] // PIECES
+    rows = [slice(i * cut, (i + 1) * cut) for i in range(PIECES)]
+    hops = [(c, c_mid, c_out), (b, b_mid, b_out)]
+    hops += [(a.at[r], a_mid.at[r], a_out.at[r]) for r in rows]
+    reads = [pltpu.make_async_copy(src, mid, sems.at[0, i]) for i, (src, mid, dst) in enumerate(hops)]
+    writes = [pltpu.make_async_copy(mid, dst, sems.at[1, i]) for i, (src, mid, dst) in enumerate(hops)]
+    for read in reads:
+        read.start()
+    for read, write in zip(reads, writes):
+        read.wait()
+        write.start()
+    for write in writes:
+        write.wait()
 
 
 def solution(mesh):
@@ -534,7 +540,7 @@
                 pltpu.VMEM((K, species), F32),
                 pltpu.VMEM((NBR, CHUNK), jnp.int32),
                 pltpu.VMEM((NBR, CHUNK), F32),
-                pltpu.VMEM((1, CHUNK), F32),
+                pltpu.VMEM((rows,), F32),
                 pltpu.VMEM((K, CHUNK), F32),
                 sems((13,)),
                 pltpu.VMEM((3 * K, rows), BF16),
@@ -569,13 +575,13 @@
                 has_side_effects=True,
                 vmem_limit_bytes=60 * 1024 * 1024,
             ),
-        )(presence, noise, factors, loadings, precision, neighbours, weights, variance.reshape(1, rows), factor_noise)
+        )(presence, noise, factors, loadings, precision, neighbours, weights, variance, factor_noise)
         return pl.pallas_call(
             write_out,
             out_shape=out_shape,
             in_specs=[hbm] * 3,
             out_specs=(hbm,) * 3,
-            scratch_shapes=[sems((6,))],
+            scratch_shapes=[pltpu.VMEM((rows, species), BF16), pltpu.VMEM((K, species), F32), pltpu.VMEM((K, rows), F32), sems((2, PIECES + 2))],
         )(*results)
 
     in_specs = (

time: 84.4 us -> 49.1 us (0.58)
  Pallas kernels: 82.3 us -> 48.3 us
  local copies, waits for them, and re-layouts: 1.33 us -> 0 us
    pallas_call x1, Pallas kernels: 36.1 us -> 2.16 us  [shards(): pl.pallas_call(write_out, out_shape=out_shape, in_specs=[hbm] * 3, out_sp...]
    reshape x1 -> x0, local copies, waits for them, and re-layouts: 1.33 us -> none  [shards(): variance.reshape(1, rows)]
where the time goes in v3:
time: 49.1 us; the launch traced here: 49 us
  Pallas kernels  48.3 us (98%)
  between operations  0.64 us (1%)
    pallas_call x1, Pallas kernels, shards(): pl.pallas_call(functools.partial(kernel, n_site, n_sp), out_shape=out_sha...  46.2 us
    pallas_call x1, Pallas kernels, shards(): pl.pallas_call(write_out, out_shape=out_shape, in_specs=[hbm] * 3, out_sp...  2.16 us

profile of v3, /device:TPU:1, one launch (start us, length us, event | category | flops | bytes accessed | tf_op | source)
XLA Modules:
  0.0 49.0 jit_solution(12360324790347855674)
XLA Ops:
  0.6 46.2 %shard_map.112 = (bf16[3584,128]{1,0:T(8,128)(2,1)}, f32[16,128]{1,0:T(8,128)}, f32[16,3584]{1,0:T(8,128)}) custom-call(s32[3584,128]{1,0:T(8,128)} %presence_hbm.1, bf16[3584,128]{1,0:T(8,128)(2,1)} %noise_hbm.1, f32[16,3584]{1,0:T(8,128)} %factors_hbm.1, f32[16,128]{1,0:T(8,128)} %loadings_hbm.1, f32[16,128]{1,0:T(8,128)} %precision_hbm.1, ...), custom_call_target="tpu_custom_call" | custom-call | tf_op jit(solution)/shard_map/pallas_call | solution.py:526
  46.8 2.2 %shard_map.113 = (bf16[3584,128]{1,0:T(8,128)(2,1)}, f32[16,128]{1,0:T(8,128)}, f32[16,3584]{1,0:T(8,128)}) custom-call(bf16[3584,128]{1,0:T(8,128)(2,1)} %get-tuple-element.6.a, f32[16,128]{1,0:T(8,128)} %get-tuple-element.7.b, f32[16,3584]{1,0:T(8,128)} %get-tuple-element.8.c), custom_call_target="tpu_custom_call" | custom-call | tf_op jit(solution)/shard_map/pallas_call | solution.py:579

commit v4 on v3

--- a/solution.py
+++ b/solution.py
@@ -120,13 +120,9 @@
     weights_hbm,
     variance_hbm,
     factor_noise_hbm,
-    utilities_hbm,
-    new_loadings_hbm,
-    new_factors_hbm,
     utilities,
     new_loadings,
     new_factors,
-    out_sems,
     presence,
     noise,
     factors,
@@ -289,8 +285,8 @@
         negative = t < 0.0
         v = jnp.where(negative, num, density * full) / jnp.where(negative, den, full - density * den)
         s = v + jnp.maximum(t, 0.0)
-        spread = jnp.maximum(1.0 - v * (v + u), 0.0)
-        draw = jnp.where(there, s, -s) + jnp.sqrt(spread) * noise[pl.ds(r0, CHUNK), :].astype(F32)
+        spread = jnp.maximum(1.0 - v * (v + u), 1e-30)
+        draw = jnp.where(there, s, -s) + spread * lax.rsqrt(spread) * noise[pl.ds(r0, CHUNK), :].astype(F32)
         d_hi, d_lo = split(draw)
         utilities[pl.ds(r0, CHUNK), :] = d_hi
         pieces = jnp.concatenate([d_hi, d_lo], axis=1)
@@ -301,7 +297,7 @@
     for piece in range(2):
         loads[2 + 2 * piece].wait()
         loads[3 + 2 * piece].wait()
-        acc = lax.fori_loop(cuts[piece] // CHUNK, cuts[piece + 1] // CHUNK, draw_step, acc)
+        acc = lax.fori_loop(cuts[piece] // CHUNK, cuts[piece + 1] // CHUNK, draw_step, acc, unroll=True)
 
     pl.semaphore_wait(barrier, len(greeted))
 
@@ -319,11 +315,9 @@
 
     loads[6].wait()
     loads[7].wait()
-    acc = lax.fori_loop(cuts[2] // CHUNK, steps, draw_step, acc)
+    acc = lax.fori_loop(cuts[2] // CHUNK, steps, draw_step, acc, unroll=True)
     cross_z[z] = blocks_sum(acc, K, species)
     started += spread_z(cross_z, cz_sems)
-    stores = [pltpu.make_async_copy(utilities, utilities_hbm, out_sems.at[0])]
-    stores[0].start()
     gram_x[x] = gather_z(gram_z, gz_sems)
     started += spread_x(gram_x, gx_sems)
 
@@ -370,8 +364,6 @@
     cross = gather_x(cross_x, cx_sems)
     fresh = solve(factor, cross, None)
     new_loadings[...] = fresh
-    stores.append(pltpu.make_async_copy(new_loadings, new_loadings_hbm, out_sems.at[1]))
-    stores[1].start()
 
     n_hi, n_lo = split(fresh)
     narrow = jnp.concatenate([n_hi, n_lo], axis=0)
@@ -470,9 +462,6 @@
     for s in range(busy):
         factors_to(fp_sems, s, s, s * CORES + (1 - core), {"sp": pair}).wait_recv()
 
-    stores.append(pltpu.make_async_copy(new_factors, new_factors_hbm, out_sems.at[2]))
-    stores[2].start()
-
     for copy in started:
         copy.wait_send()
     for s in range(busy):
@@ -488,21 +477,13 @@
             t = (y + d) % ny
             factors_to(fy_sems, d, y, y * CORES + core, {"sp": t * CORES + core}).wait_send()
 
-    for store in stores:
-        store.wait()
-
-
-def write_out(a, b, c, a_out, b_out, c_out, a_mid, b_mid, c_mid, sems):
+
+def write_out(a, b, c, a_out, b_out, c_out, sems):
     cut = a.shape[0] // PIECES
     rows = [slice(i * cut, (i + 1) * cut) for i in range(PIECES)]
-    hops = [(c, c_mid, c_out), (b, b_mid, b_out)]
-    hops += [(a.at[r], a_mid.at[r], a_out.at[r]) for r in rows]
-    reads = [pltpu.make_async_copy(src, mid, sems.at[0, i]) for i, (src, mid, dst) in enumerate(hops)]
-    writes = [pltpu.make_async_copy(mid, dst, sems.at[1, i]) for i, (src, mid, dst) in enumerate(hops)]
-    for read in reads:
-        read.start()
-    for read, write in zip(reads, writes):
-        read.wait()
+    pairs = [(c, c_out), (b, b_out)] + [(a.at[r], a_out.at[r]) for r in rows]
+    writes = [pltpu.make_async_copy(src, dst, sems.at[i]) for i, (src, dst) in enumerate(pairs)]
+    for write in writes:
         write.start()
     for write in writes:
         write.wait()
@@ -516,6 +497,7 @@
     def shards(presence, noise, factors, loadings, precision, neighbours, weights, variance, factor_noise):
         rows, species = presence.shape
         assert rows == busy * CORES * CHUNK and species == 128
+        vmem = pl.BlockSpec(memory_space=pltpu.VMEM)
         hbm = pl.BlockSpec(memory_space=pltpu.HBM)
         sems = pltpu.SemaphoreType.DMA
         out_shape = (
@@ -525,14 +507,10 @@
         )
         results = pl.pallas_call(
             functools.partial(kernel, n_site, n_sp),
-            out_shape=out_shape,
+            out_shape=tuple(pltpu.VMEM(v.shape, v.dtype) for v in out_shape),
             in_specs=[hbm] * 9,
-            out_specs=(hbm,) * 3,
+            out_specs=(vmem,) * 3,
             scratch_shapes=[
-                pltpu.VMEM((rows, species), BF16),
-                pltpu.VMEM((K, species), F32),
-                pltpu.VMEM((K, rows), F32),
-                sems((3,)),
                 pltpu.VMEM((rows, species), jnp.int32),
                 pltpu.VMEM((rows, species), BF16),
                 pltpu.VMEM((K, rows), F32),
@@ -579,10 +557,10 @@
         return pl.pallas_call(
             write_out,
             out_shape=out_shape,
-            in_specs=[hbm] * 3,
+            in_specs=[vmem] * 3,
             out_specs=(hbm,) * 3,
-            scratch_shapes=[pltpu.VMEM((rows, species), BF16), pltpu.VMEM((K, species), F32), pltpu.VMEM((K, rows), F32), sems((2, PIECES + 2))],
-        )(*results)
+            scratch_shapes=[sems((PIECES + 2,))],
+        )(*[pltpu.with_memory_space_constraint(v, pltpu.VMEM) for v in results])
 
     in_specs = (
         P("site", "sp"),

time: 49.1 us -> 45.6 us (0.929)
  Pallas kernels: 48.3 us -> 44.8 us
    pallas_call x2, Pallas kernels: 48.3 us -> 44.8 us  [the longest x1 43.8 us: shards(): pl.pallas_call(functools.partial(kernel, n_site, n_sp), out_shape=tuple((...]
where the time goes in v4:
time: 45.6 us; the launch traced here: 45.5 us
  Pallas kernels  44.8 us (98%)
  between operations  0.64 us (1%)
    pallas_call x1, Pallas kernels, shards(): pl.pallas_call(functools.partial(kernel, n_site, n_sp), out_shape=tuple((...  43.8 us
    pallas_call x1, Pallas kernels, shards(): pl.pallas_call(write_out, out_shape=out_shape, in_specs=[vmem] * 3, out_s...  1.05 us

profile of v4, /device:TPU:1, one launch (start us, length us, event | category | flops | bytes accessed | tf_op | source)
XLA Modules:
  0.0 45.5 jit_solution(9716676212401615630)
XLA Ops:
  0.6 43.8 %shard_map.112 = (bf16[3584,128]{1,0:T(8,128)(2,1)S(1)}, f32[16,128]{1,0:T(8,128)S(1)}, f32[16,3584]{1,0:T(8,128)S(1)}) custom-call(s32[3584,128]{1,0:T(8,128)} %presence_hbm.1, bf16[3584,128]{1,0:T(8,128)(2,1)} %noise_hbm.1, f32[16,3584]{1,0:T(8,128)} %factors_hbm.1, f32[16,128]{1,0:T(8,128)} %loadings_hbm.1, f32[16,128]{1,0:T(8,128)} %precision_hbm.1, ...), custom_call_target="tpu_custom_call" | custom-call | tf_op jit(solution)/shard_map/pallas_call | solution.py:508
  44.4 1.0 %shard_map.113 = (bf16[3584,128]{1,0:T(8,128)(2,1)}, f32[16,128]{1,0:T(8,128)}, f32[16,3584]{1,0:T(8,128)}) custom-call(bf16[3584,128]{1,0:T(8,128)(2,1)S(1)} %get-tuple-element.6.a, f32[16,128]{1,0:T(8,128)S(1)} %get-tuple-element.7.b, f32[16,3584]{1,0:T(8,128)S(1)} %get-tuple-element.8.c), custom_call_target="tpu_custom_call" | custom-call | tf_op jit(solution)/shard_map/pallas_call | solution.py:557

commit v5 on v4

--- a/solution.py
+++ b/solution.py
@@ -60,48 +60,53 @@
         else:
             top.append(None)
             bot.append(column[HALF:] + diag)
-    scales = []
+    inv_top = [jnp.where(row == k, 1.0, 0.0) if k < HALF else jnp.zeros((HALF, width), F32) for k in range(K)]
+    inv_bot = [None if k < HALF else jnp.where(row == k - HALF, 1.0, 0.0) for k in range(K)]
+    pivots = []
     for j in range(K):
         d = top[j][j : j + 1] if j < HALF else bot[j][j - HALF : j - HALF + 1]
         r = lax.rsqrt(d)
-        scales.append(r)
+        pivots.append(d * r)
         bot[j] = bot[j] * r
+        inv_top[j] = inv_top[j] * r
         if j < HALF:
             top[j] = top[j] * r
+        else:
+            inv_bot[j] = inv_bot[j] * r
         for k in range(j + 1, K):
             if k < HALF:
                 s = top[j][k : k + 1]
                 top[k] = top[k] - top[j] * s
                 bot[k] = bot[k] - bot[j] * s
             else:
-                bot[k] = bot[k] - bot[j] * bot[j][k - HALF : k - HALF + 1]
-    return top, bot, scales
-
-
-def solve(factor, rhs, noise):
-    top, bot, scales = factor
-    rt, rb = rhs[:HALF], rhs[HALF:]
-    middle = []
+                s = bot[j][k - HALF : k - HALF + 1]
+                bot[k] = bot[k] - bot[j] * s
+            inv_top[k] = inv_top[k] - inv_top[j] * s
+            if j >= HALF:
+                inv_bot[k] = inv_bot[k] - inv_bot[j] * s
+    return inv_top, inv_bot, pivots
+
+
+def apply_pivots(pivots, noise):
+    row = lax.broadcasted_iota(jnp.int32, noise.shape, 0)
+    acc = jnp.zeros_like(noise)
     for j in range(K):
-        y = (rt[j : j + 1] if j < HALF else rb[j - HALF : j - HALF + 1]) * scales[j]
-        if noise is not None:
-            y = y + noise[j : j + 1]
-        middle.append(y)
-        if j < HALF:
-            rt = rt - top[j] * y
-        rb = rb - bot[j] * y
-    row = lax.broadcasted_iota(jnp.int32, rt.shape, 0)
-    xt, xb = jnp.zeros_like(rt), jnp.zeros_like(rt)
-    for j in range(K - 1, -1, -1):
-        terms = bot[j] * xb
-        if j < HALF:
-            terms = terms + top[j] * xt
-        x = (middle[j] - jnp.sum(terms, axis=0, keepdims=True)) * scales[j]
-        if j < HALF:
-            xt = jnp.where(row == j, x, xt)
-        else:
-            xb = jnp.where(row == j - HALF, x, xb)
-    return jnp.concatenate([xt, xb], axis=0)
+        acc = jnp.where(row == j, pivots[j], acc)
+    return acc * noise
+
+
+def solve(inv_top, inv_bot, rhs):
+    top, bot = rhs[:HALF], rhs[HALF:]
+    x_top = x_bot = None
+    for j in range(K):
+        terms = inv_top[j] * top
+        if j >= HALF:
+            terms = terms + inv_bot[j] * bot
+        y = jnp.sum(terms, axis=0, keepdims=True)
+        x_top = inv_top[j] * y if x_top is None else x_top + inv_top[j] * y
+        if j >= HALF:
+            x_bot = inv_bot[j] * y if x_bot is None else x_bot + inv_bot[j] * y
+    return jnp.concatenate([x_top, x_bot], axis=0)
 
 
 def far_first(n):
@@ -141,9 +146,7 @@
     gram_x,
     cross_z,
     cross_x,
-    lgram_mine,
-    lgram_pair,
-    lgram_y,
+    lgram_all,
     pull_out,
     pull_pair,
     pull_mine,
@@ -153,7 +156,6 @@
     gx_sems,
     cz_sems,
     cx_sems,
-    lp_sems,
     ly_sems,
     pp_sems,
     py_sems,
@@ -179,61 +181,11 @@
     def z_peer(d):
         return x * Z + (z + d) % Z
 
+    def sp_peer(o):
+        return ((y + o // CORES) % ny) * CORES + (core + o) % CORES
+
     def x_peer(d):
         return ((x + d) % nx) * Z + z
-
-    barrier = pltpu.get_barrier_semaphore()
-    greeted = [{"site": z_peer(d)} for d in range(1, Z)]
-    greeted += [{"site": x_peer(d)} for d in range(1, nx)]
-    greeted += [{"site": ahead}, {"site": behind}]
-    greeted += [{"sp": ((y + d) % ny) * CORES + core} for d in range(1, ny)]
-    greeted += [{"sp": pair}]
-    for peer in greeted:
-        pl.semaphore_signal(barrier, inc=1, device_id=peer, device_id_type=MESH)
-
-    def remote(src, dst, sems, send, recv, peer):
-        return pltpu.make_async_remote_copy(
-            src_ref=src,
-            dst_ref=dst,
-            send_sem=sems.at[0, send],
-            recv_sem=sems.at[1, recv],
-            device_id=peer,
-            device_id_type=MESH,
-        )
-
-    def spread_z(buf, sems):
-        copies = []
-        for d in far_first(Z):
-            copy = remote(buf.at[z], buf.at[z], sems, d, d, {"site": z_peer(d)})
-            copy.start()
-            copies.append(copy)
-        return copies
-
-    def spread_x(buf, sems):
-        copies = []
-        for d in far_first(nx):
-            copy = remote(buf.at[x], buf.at[x], sems, d, d, {"site": x_peer(d)})
-            copy.start()
-            copies.append(copy)
-        return copies
-
-    def gather_z(buf, sems):
-        for d in range(1, Z):
-            s = (z + Z - d) % Z
-            remote(buf.at[s], buf.at[s], sems, d, d, {"site": z_peer(d)}).wait_recv()
-        acc = buf[0]
-        for s in range(1, Z):
-            acc = acc + buf[s]
-        return acc
-
-    def gather_x(buf, sems):
-        for d in range(1, nx):
-            s = (x + nx - d) % nx
-            remote(buf.at[s], buf.at[s], sems, d, d, {"site": x_peer(d)}).wait_recv()
-        acc = buf[0]
-        for s in range(1, nx):
-            acc = acc + buf[s]
-        return acc
 
     chunk = jnp.minimum(sp, CORES * busy - 1)
     c0 = pl.multiple_of(chunk * CHUNK, CHUNK)
@@ -252,6 +204,59 @@
     loads = [pltpu.make_async_copy(a, b, in_sems.at[i]) for i, (a, b) in enumerate(loads)]
     for load in loads:
         load.start()
+
+    barrier = pltpu.get_barrier_semaphore()
+    greeted = [{"site": z_peer(d)} for d in range(1, Z)]
+    greeted += [{"site": x_peer(d)} for d in range(1, nx)]
+    greeted += [{"site": ahead}, {"site": behind}]
+    greeted += [{"sp": sp_peer(o)} for o in range(1, n_sp)]
+    for peer in greeted:
+        pl.semaphore_signal(barrier, inc=1, device_id=peer, device_id_type=MESH)
+
+    def remote(src, dst, sems, send, recv, peer):
+        return pltpu.make_async_remote_copy(
+            src_ref=src,
+            dst_ref=dst,
+            send_sem=sems.at[0, send],
+            recv_sem=sems.at[1, recv],
+            device_id=peer,
+            device_id_type=MESH,
+        )
+
+    def spread_z(buf, sems):
+        copies = []
+        for d in far_first(Z):
+            copy = remote(buf.at[z], buf.at[z], sems, d, d, {"site": z_peer(d)})
+            copy.start()
+            copies.append(copy)
+        return copies
+
+    def spread_x(buf, sems):
+        copies = []
+        for d in far_first(nx):
+            copy = remote(buf.at[x], buf.at[x], sems, d, d, {"site": x_peer(d)})
+            copy.start()
+            copies.append(copy)
+        return copies
+
+    def gather_z(buf, sems):
+        for d in range(1, Z):
+            s = (z + Z - d) % Z
+            remote(buf.at[s], buf.at[s], sems, d, d, {"site": z_peer(d)}).wait_recv()
+        acc = buf[0]
+        for s in range(1, Z):
+            acc = acc + buf[s]
+        return acc
+
+    def gather_x(buf, sems):
+        for d in range(1, nx):
+            s = (x + nx - d) % nx
+            remote(buf.at[s], buf.at[s], sems, d, d, {"site": x_peer(d)}).wait_recv()
+        acc = buf[0]
+        for s in range(1, nx):
+            acc = acc + buf[s]
+        return acc
+
     started = []
 
     loads[0].wait()
@@ -264,13 +269,6 @@
     window[:, RIM:] = f
     l_hi, l_lo = split(loadings[...])
     ls = jnp.concatenate([l_hi, l_hi, l_lo], axis=0)
-
-    both = jnp.concatenate([hi, lo], axis=0)
-    products = dot(both, both, ((1,), (1,)))
-    gram_part = blocks_sum(products, K, K)
-    zeros = jnp.zeros((K, species), F32)
-    gram_z[z] = zeros
-    gram_z[z, :, 0:K] = gram_part
 
     def draw_step(i, acc):
         r0 = pl.multiple_of(i * CHUNK, CHUNK)
@@ -299,6 +297,12 @@
         loads[3 + 2 * piece].wait()
         acc = lax.fori_loop(cuts[piece] // CHUNK, cuts[piece + 1] // CHUNK, draw_step, acc, unroll=True)
 
+    products = dot(fs[0:32, :], fs[0:32, :], ((1,), (1,)))
+    gram_part = blocks_sum(products, K, K)
+    zeros = jnp.zeros((K, species), F32)
+    gram_z[z] = zeros
+    gram_z[z, :, 0:K] = gram_part
+
     pl.semaphore_wait(barrier, len(greeted))
 
     rim = remote(
@@ -359,20 +363,21 @@
     started += spread_x(cross_x, cx_sems)
 
     gram = gather_x(gram_x, gx_sems)[:, 0:K]
-    factor = cholesky(gram, [precision[k : k + 1, :] for k in range(K)])
+    inv_top, inv_bot, _ = cholesky(gram, [precision[k : k + 1, :] for k in range(K)])
 
     cross = gather_x(cross_x, cx_sems)
-    fresh = solve(factor, cross, None)
+    fresh = solve(inv_top, inv_bot, cross)
     new_loadings[...] = fresh
 
     n_hi, n_lo = split(fresh)
     narrow = jnp.concatenate([n_hi, n_lo], axis=0)
     lgram_part = blocks_sum(dot(narrow, narrow, ((1,), (1,))), K, K)
-    lgram_mine[...] = zeros
-    lgram_mine[:, 0:K] = lgram_part
-    copy = remote(lgram_mine, lgram_pair, lp_sems, 0, 0, {"sp": pair})
-    copy.start()
-    started.append(copy)
+    lgram_all[sp] = zeros
+    lgram_all[sp, :, 0:K] = lgram_part
+    for o in sorted(range(1, n_sp), key=lambda o: -min(o // CORES, ny - o // CORES)):
+        copy = remote(lgram_all.at[sp], lgram_all.at[sp], ly_sems, o, o, {"sp": sp_peer(o)})
+        copy.start()
+        started.append(copy)
 
     zero = jnp.zeros_like(n_hi)
     wide = jnp.concatenate(
@@ -389,25 +394,18 @@
     order.remove(busy)
     order.append(busy)
     for e in order:
-        t = (y + e) % busy
-        pull_out[e - 1] = pull_of(t, 1 - core)
+        pull_out[e - 1] = pull_of((y + e) % busy, 1 - core)
+    for e in order:
         copy = remote(pull_out.at[e - 1], pull_pair.at[e - 1], pp_sems, e - 1, e - 1, {"sp": pair})
         copy.start()
         started.append(copy)
 
-    remote(lgram_mine, lgram_pair, lp_sems, 0, 0, {"sp": pair}).wait_recv()
-    lgram_y[y] = lgram_mine[...] + lgram_pair[...]
-    for d in far_first(ny):
-        peer = {"sp": ((y + d) % ny) * CORES + core}
-        copy = remote(lgram_y.at[y], lgram_y.at[y], ly_sems, d, d, peer)
-        copy.start()
-        started.append(copy)
-
+    for e in order:
+        pull_mine[e - 1] = pull_of((y + e) % busy, core)
     for e in order:
         t = (y + e) % busy
-        part = pull_of(t, core)
         remote(pull_out.at[e - 1], pull_pair.at[e - 1], pp_sems, e - 1, e - 1, {"sp": pair}).wait_recv()
-        pull_mine[e - 1] = part + pull_pair[e - 1]
+        pull_mine[e - 1] += pull_pair[e - 1]
         copy = remote(pull_mine.at[e - 1], pull_y.at[y], py_sems, e, y, {"sp": t * CORES + core})
         if e < busy:
             copy.start()
@@ -420,10 +418,9 @@
 
             last_pull = copy
 
-    for d in range(1, ny):
-        s = (y + ny - d) % ny
-        peer = {"sp": ((y + d) % ny) * CORES + core}
-        remote(lgram_y.at[s], lgram_y.at[s], ly_sems, d, d, peer).wait_recv()
+    for o in range(1, n_sp):
+        s = ((y + ny - o // CORES) % ny) * CORES + (core + o) % CORES
+        remote(lgram_all.at[s], lgram_all.at[s], ly_sems, o, o, {"sp": s}).wait_recv()
 
     def factors_to(sems, send, recv, index, peer):
         lanes = pl.ds(pl.multiple_of(index * CHUNK, CHUNK), CHUNK)
@@ -431,22 +428,25 @@
 
     @pl.when(y < busy)
     def _():
-        lgram = lgram_y[0]
-        for s in range(1, ny):
-            lgram = lgram + lgram_y[s]
-        site_factor = cholesky(lgram[:, 0:K], [inverse] * K)
-        total = pull_mine[busy - 1] + shift
+        lgram = lgram_all[0]
+        for s in range(1, n_sp):
+            lgram = lgram + lgram_all[s]
+        site_top, site_bot, pivots = cholesky(lgram[:, 0:K], [inverse] * K)
+        total = pull_mine[busy - 1] + (shift + apply_pivots(pivots, factor_noise[...]))
         for d in range(1, ny):
             s = (y + d) % ny
             remote(pull_y.at[s], pull_y.at[s], py_sems, 0, s, {"sp": s * CORES + core}).wait_recv()
             total = total + pull_y[s]
-        result = solve(site_factor, total, factor_noise[...])
+        result = solve(site_top, site_bot, total)
         new_factors[:, pl.ds(c0, CHUNK)] = result
         for d in far_first(ny):
             t = (y + d) % ny
             factors_to(fy_sems, d, y, y * CORES + core, {"sp": t * CORES + core}).start()
         factors_to(fp_sems, y, y, y * CORES + core, {"sp": pair}).start()
 
+    for copy in started:
+        copy.wait_send()
+
     for e in order[busy - 2 :: -1] + [busy]:
         s = (y + busy - e) % busy
 
@@ -462,8 +462,6 @@
     for s in range(busy):
         factors_to(fp_sems, s, s, s * CORES + (1 - core), {"sp": pair}).wait_recv()
 
-    for copy in started:
-        copy.wait_send()
     for s in range(busy):
         factors_to(fp_sems, s, s, s * CORES + core, {"sp": pair}).wait_send()
 
@@ -529,9 +527,7 @@
                 pltpu.VMEM((nx, K, species), F32),
                 pltpu.VMEM((Z, K, species), F32),
                 pltpu.VMEM((nx, K, species), F32),
-                pltpu.VMEM((K, species), F32),
-                pltpu.VMEM((K, species), F32),
-                pltpu.VMEM((ny, K, species), F32),
+                pltpu.VMEM((n_sp, K, species), F32),
                 pltpu.VMEM((busy, K, CHUNK), F32),
                 pltpu.VMEM((busy, K, CHUNK), F32),
                 pltpu.VMEM((busy, K, CHUNK), F32),
@@ -541,8 +537,7 @@
                 sems((2, nx)),
                 sems((2, Z)),
                 sems((2, nx)),
-                sems((2, 1)),
-                sems((2, ny)),
+                sems((2, n_sp)),
                 sems((2, busy)),
                 sems((2, ny)),
                 sems((2, ny)),

time: 45.6 us -> 45.1 us (0.989)
  Pallas kernels: 44.8 us -> 44.3 us
    pallas_call x1, Pallas kernels: 43.8 us -> 43.3 us  [shards(): pl.pallas_call(functools.partial(kernel, n_site, n_sp), out_shape=tuple((...]
where the time goes in v5:
time: 45.1 us; the launch traced here: 45 us
  Pallas kernels  44.3 us (98%)
  between operations  0.64 us (1%)
    pallas_call x1, Pallas kernels, shards(): pl.pallas_call(functools.partial(kernel, n_site, n_sp), out_shape=tuple((...  43.3 us
    pallas_call x1, Pallas kernels, shards(): pl.pallas_call(write_out, out_shape=out_shape, in_specs=[vmem] * 3, out_s...  1.05 us

profile of v5, /device:TPU:1, one launch (start us, length us, event | category | flops | bytes accessed | tf_op | source)
XLA Modules:
  0.0 45.0 jit_solution(17628487090096799681)
XLA Ops:
  0.6 43.3 %shard_map.112 = (bf16[3584,128]{1,0:T(8,128)(2,1)S(1)}, f32[16,128]{1,0:T(8,128)S(1)}, f32[16,3584]{1,0:T(8,128)S(1)}) custom-call(s32[3584,128]{1,0:T(8,128)} %presence_hbm.1, bf16[3584,128]{1,0:T(8,128)(2,1)} %noise_hbm.1, f32[16,3584]{1,0:T(8,128)} %factors_hbm.1, f32[16,128]{1,0:T(8,128)} %loadings_hbm.1, f32[16,128]{1,0:T(8,128)} %precision_hbm.1, ...), custom_call_target="tpu_custom_call" | custom-call | tf_op jit(solution)/shard_map/pallas_call | solution.py:506
  43.9 1.0 %shard_map.113 = (bf16[3584,128]{1,0:T(8,128)(2,1)}, f32[16,128]{1,0:T(8,128)}, f32[16,3584]{1,0:T(8,128)}) custom-call(bf16[3584,128]{1,0:T(8,128)(2,1)S(1)} %get-tuple-element.6.a, f32[16,128]{1,0:T(8,128)S(1)} %get-tuple-element.7.b, f32[16,3584]{1,0:T(8,128)S(1)} %get-tuple-element.8.c), custom_call_target="tpu_custom_call" | custom-call | tf_op jit(solution)/shard_map/pallas_call | solution.py:552

commit v6 on v5

--- a/solution.py
+++ b/solution.py
@@ -109,6 +109,13 @@
     return jnp.concatenate([x_top, x_bot], axis=0)
 
 
+def total_of(ref, count):
+    parts = [ref[i] for i in range(count)]
+    while len(parts) > 1:
+        parts = [a + b for a, b in zip(parts[::2], parts[1::2])] + parts[len(parts) // 2 * 2 :]
+    return parts[0]
+
+
 def far_first(n):
     return sorted(range(1, n), key=lambda d: -min(d, n - d))
 
@@ -144,8 +151,7 @@
     onehot,
     gram_z,
     gram_x,
-    cross_z,
-    cross_x,
+    cross_all,
     lgram_all,
     pull_out,
     pull_pair,
@@ -154,8 +160,7 @@
     rim_sems,
     gz_sems,
     gx_sems,
-    cz_sems,
-    cx_sems,
+    cross_sems,
     ly_sems,
     pp_sems,
     py_sems,
@@ -176,10 +181,16 @@
     y, core = sp // CORES, sp % CORES
     pair = y * CORES + (1 - core)
     ahead = (site + 1) % n_site
-    behind = (site + n_site - 1) % n_site
 
     def z_peer(d):
         return x * Z + (z + d) % Z
+
+    def site_peer(o, sign=1):
+        return ((x + nx + sign * (o // Z)) % nx) * Z + (z + Z + sign * (o % Z)) % Z
+
+    def hops(o):
+        dx, dz = o // Z, o % Z
+        return min(dx, nx - dx) + min(dz, Z - dz)
 
     def sp_peer(o):
         return ((y + o // CORES) % ny) * CORES + (core + o) % CORES
@@ -206,9 +217,7 @@
         load.start()
 
     barrier = pltpu.get_barrier_semaphore()
-    greeted = [{"site": z_peer(d)} for d in range(1, Z)]
-    greeted += [{"site": x_peer(d)} for d in range(1, nx)]
-    greeted += [{"site": ahead}, {"site": behind}]
+    greeted = [{"site": (site + d) % n_site} for d in range(1, n_site)]
     greeted += [{"sp": sp_peer(o)} for o in range(1, n_sp)]
     for peer in greeted:
         pl.semaphore_signal(barrier, inc=1, device_id=peer, device_id_type=MESH)
@@ -320,8 +329,11 @@
     loads[6].wait()
     loads[7].wait()
     acc = lax.fori_loop(cuts[2] // CHUNK, steps, draw_step, acc, unroll=True)
-    cross_z[z] = blocks_sum(acc, K, species)
-    started += spread_z(cross_z, cz_sems)
+    cross_all[site] = blocks_sum(acc, K, species)
+    for o in sorted(range(1, n_site), key=lambda o: -hops(o)):
+        copy = remote(cross_all.at[site], cross_all.at[site], cross_sems, o, o, {"site": site_peer(o)})
+        copy.start()
+        started.append(copy)
     gram_x[x] = gather_z(gram_z, gz_sems)
     started += spread_x(gram_x, gx_sems)
 
@@ -359,13 +371,13 @@
     inverse = 1.0 / variance[pl.ds(c0, CHUNK)].reshape(1, CHUNK)
     shift = prior * inverse
 
-    cross_x[x] = gather_z(cross_z, cz_sems)
-    started += spread_x(cross_x, cx_sems)
-
     gram = gather_x(gram_x, gx_sems)[:, 0:K]
     inv_top, inv_bot, _ = cholesky(gram, [precision[k : k + 1, :] for k in range(K)])
 
-    cross = gather_x(cross_x, cx_sems)
+    for o in sorted(range(1, n_site), key=hops):
+        s = site_peer(o, -1)
+        remote(cross_all.at[s], cross_all.at[s], cross_sems, o, o, {"site": s}).wait_recv()
+    cross = total_of(cross_all, n_site)
     fresh = solve(inv_top, inv_bot, cross)
     new_loadings[...] = fresh
 
@@ -428,9 +440,7 @@
 
     @pl.when(y < busy)
     def _():
-        lgram = lgram_all[0]
-        for s in range(1, n_sp):
-            lgram = lgram + lgram_all[s]
+        lgram = total_of(lgram_all, n_sp)
         site_top, site_bot, pivots = cholesky(lgram[:, 0:K], [inverse] * K)
         total = pull_mine[busy - 1] + (shift + apply_pivots(pivots, factor_noise[...]))
         for d in range(1, ny):
@@ -525,8 +535,7 @@
                 pltpu.VMEM((WINDOW, CHUNK), F32),
                 pltpu.VMEM((Z, K, species), F32),
                 pltpu.VMEM((nx, K, species), F32),
-                pltpu.VMEM((Z, K, species), F32),
-                pltpu.VMEM((nx, K, species), F32),
+                pltpu.VMEM((n_site, K, species), F32),
                 pltpu.VMEM((n_sp, K, species), F32),
                 pltpu.VMEM((busy, K, CHUNK), F32),
                 pltpu.VMEM((busy, K, CHUNK), F32),
@@ -535,8 +544,7 @@
                 sems((2, 1)),
                 sems((2, Z)),
                 sems((2, nx)),
-                sems((2, Z)),
-                sems((2, nx)),
+                sems((2, n_site)),
                 sems((2, n_sp)),
                 sems((2, busy)),
                 sems((2, ny)),

time: 45.1 us -> 46.7 us (1.035)
  Pallas kernels: 44.3 us -> 45.9 us
    pallas_call x1, Pallas kernels: 43.3 us -> 44.9 us  [shards(): pl.pallas_call(functools.partial(kernel, n_site, n_sp), out_shape=tuple((...]
where the time goes in v6:
time: 46.7 us; the launch traced here: 46.5 us
  Pallas kernels  45.9 us (98%)
  between operations  0.64 us (1%)
    pallas_call x1, Pallas kernels, shards(): pl.pallas_call(functools.partial(kernel, n_site, n_sp), out_shape=tuple((...  44.9 us
    pallas_call x1, Pallas kernels, shards(): pl.pallas_call(write_out, out_shape=out_shape, in_specs=[vmem] * 3, out_s...  1.05 us

profile of v6, /device:TPU:1, one launch (start us, length us, event | category | flops | bytes accessed | tf_op | source)
XLA Modules:
  0.0 46.5 jit_solution(6321499314608483144)
XLA Ops:
  0.6 44.9 %shard_map.112 = (bf16[3584,128]{1,0:T(8,128)(2,1)S(1)}, f32[16,128]{1,0:T(8,128)S(1)}, f32[16,3584]{1,0:T(8,128)S(1)}) custom-call(s32[3584,128]{1,0:T(8,128)} %presence_hbm.1, bf16[3584,128]{1,0:T(8,128)(2,1)} %noise_hbm.1, f32[16,3584]{1,0:T(8,128)} %factors_hbm.1, f32[16,128]{1,0:T(8,128)} %loadings_hbm.1, f32[16,128]{1,0:T(8,128)} %precision_hbm.1, ...), custom_call_target="tpu_custom_call" | custom-call | tf_op jit(solution)/shard_map/pallas_call | solution.py:516
  45.5 1.0 %shard_map.113 = (bf16[3584,128]{1,0:T(8,128)(2,1)}, f32[16,128]{1,0:T(8,128)}, f32[16,3584]{1,0:T(8,128)}) custom-call(bf16[3584,128]{1,0:T(8,128)(2,1)S(1)} %get-tuple-element.6.a, f32[16,128]{1,0:T(8,128)S(1)} %get-tuple-element.7.b, f32[16,3584]{1,0:T(8,128)S(1)} %get-tuple-element.8.c), custom_call_target="tpu_custom_call" | custom-call | tf_op jit(solution)/shard_map/pallas_call | solution.py:560

commit v7 on v5

--- a/solution.py
+++ b/solution.py
@@ -53,13 +53,13 @@
     top, bot = [], []
     for k in range(K):
         diag = jnp.where(row == k % HALF, extra[k], 0.0)
-        column = base[:, k : k + 1]
+        lower = base[:, K + k : K + k + 1]
         if k < HALF:
-            top.append(column[:HALF] + diag)
-            bot.append(column[HALF:] + jnp.zeros_like(diag))
+            top.append(base[:, k : k + 1] + diag)
+            bot.append(lower + jnp.zeros_like(diag))
         else:
             top.append(None)
-            bot.append(column[HALF:] + diag)
+            bot.append(lower + diag)
     inv_top = [jnp.where(row == k, 1.0, 0.0) if k < HALF else jnp.zeros((HALF, width), F32) for k in range(K)]
     inv_bot = [None if k < HALF else jnp.where(row == k - HALF, 1.0, 0.0) for k in range(K)]
     pivots = []
@@ -202,7 +202,7 @@
         (factor_noise_hbm.at[:, mine], factor_noise),
     ]
     loads = [pltpu.make_async_copy(a, b, in_sems.at[i]) for i, (a, b) in enumerate(loads)]
-    for load in loads:
+    for load in loads[:6]:
         load.start()
 
     barrier = pltpu.get_barrier_semaphore()
@@ -261,6 +261,8 @@
 
     loads[0].wait()
     loads[1].wait()
+    for load in loads[6:]:
+        load.start()
     f = factors[...]
     hi, lo = split(f)
     fs[0:16, :] = hi
@@ -299,9 +301,10 @@
 
     products = dot(fs[0:32, :], fs[0:32, :], ((1,), (1,)))
     gram_part = blocks_sum(products, K, K)
-    zeros = jnp.zeros((K, species), F32)
+    zeros = jnp.zeros((HALF, 128), F32)
     gram_z[z] = zeros
-    gram_z[z, :, 0:K] = gram_part
+    gram_z[z, :, 0:K] = gram_part[:HALF]
+    gram_z[z, :, K : 2 * K] = gram_part[HALF:]
 
     pl.semaphore_wait(barrier, len(greeted))
 
@@ -314,8 +317,12 @@
         {"site": ahead},
     )
     started += spread_z(gram_z, gz_sems)
-    rim.start()
-    started.append(rim)
+    reached = sp < RIM // CHUNK
+
+    @pl.when(reached)
+    def _():
+        rim.start()
+
 
     loads[6].wait()
     loads[7].wait()
@@ -342,7 +349,11 @@
         return carry
 
     lax.fori_loop(0, NBR, mark, 0)
-    rim.wait_recv()
+
+    @pl.when(reached)
+    def _():
+        rim.wait()
+
 
     def gather_step(b, acc):
         r0 = pl.multiple_of(b * 256, 256)
@@ -362,7 +373,7 @@
     cross_x[x] = gather_z(cross_z, cz_sems)
     started += spread_x(cross_x, cx_sems)
 
-    gram = gather_x(gram_x, gx_sems)[:, 0:K]
+    gram = gather_x(gram_x, gx_sems)
     inv_top, inv_bot, _ = cholesky(gram, [precision[k : k + 1, :] for k in range(K)])
 
     cross = gather_x(cross_x, cx_sems)
@@ -372,13 +383,6 @@
     n_hi, n_lo = split(fresh)
     narrow = jnp.concatenate([n_hi, n_lo], axis=0)
     lgram_part = blocks_sum(dot(narrow, narrow, ((1,), (1,))), K, K)
-    lgram_all[sp] = zeros
-    lgram_all[sp, :, 0:K] = lgram_part
-    for o in sorted(range(1, n_sp), key=lambda o: -min(o // CORES, ny - o // CORES)):
-        copy = remote(lgram_all.at[sp], lgram_all.at[sp], ly_sems, o, o, {"sp": sp_peer(o)})
-        copy.start()
-        started.append(copy)
-
     zero = jnp.zeros_like(n_hi)
     wide = jnp.concatenate(
         [jnp.concatenate([n_hi, n_hi], axis=1), jnp.concatenate([n_lo, zero], axis=1)],
@@ -395,8 +399,16 @@
     order.append(busy)
     for e in order:
         pull_out[e - 1] = pull_of((y + e) % busy, 1 - core)
+    lgram_all[sp] = zeros
+    lgram_all[sp, :, 0:K] = lgram_part[:HALF]
+    lgram_all[sp, :, K : 2 * K] = lgram_part[HALF:]
     for e in order:
         copy = remote(pull_out.at[e - 1], pull_pair.at[e - 1], pp_sems, e - 1, e - 1, {"sp": pair})
+        copy.start()
+        started.append(copy)
+
+    for o in sorted(range(1, n_sp), key=lambda o: -min(o // CORES, ny - o // CORES)):
+        copy = remote(lgram_all.at[sp], lgram_all.at[sp], ly_sems, o, o, {"sp": sp_peer(o)})
         copy.start()
         started.append(copy)
 
@@ -431,7 +443,7 @@
         lgram = lgram_all[0]
         for s in range(1, n_sp):
             lgram = lgram + lgram_all[s]
-        site_top, site_bot, pivots = cholesky(lgram[:, 0:K], [inverse] * K)
+        site_top, site_bot, pivots = cholesky(lgram, [inverse] * K)
         total = pull_mine[busy - 1] + (shift + apply_pivots(pivots, factor_noise[...]))
         for d in range(1, ny):
             s = (y + d) % ny
@@ -523,11 +535,11 @@
                 pltpu.VMEM((rows, 2 * species), BF16),
                 pltpu.VMEM((K, RIM + rows), F32),
                 pltpu.VMEM((WINDOW, CHUNK), F32),
+                pltpu.VMEM((Z, HALF, 128), F32),
+                pltpu.VMEM((nx, HALF, 128), F32),
                 pltpu.VMEM((Z, K, species), F32),
                 pltpu.VMEM((nx, K, species), F32),
-                pltpu.VMEM((Z, K, species), F32),
-                pltpu.VMEM((nx, K, species), F32),
-                pltpu.VMEM((n_sp, K, species), F32),
+                pltpu.VMEM((n_sp, HALF, 128), F32),
                 pltpu.VMEM((busy, K, CHUNK), F32),
                 pltpu.VMEM((busy, K, CHUNK), F32),
                 pltpu.VMEM((busy, K, CHUNK), F32),

time: 45.1 us -> 43.3 us (0.960)
  Pallas kernels: 44.3 us -> 42.5 us
    pallas_call x1, Pallas kernels: 43.3 us -> 41.5 us  [shards(): pl.pallas_call(functools.partial(kernel, n_site, n_sp), out_shape=tuple((...]
where the time goes in v7:
time: 43.3 us; the launch traced here: 43.2 us
  Pallas kernels  42.5 us (98%)
  between operations  0.64 us (1%)
    pallas_call x1, Pallas kernels, shards(): pl.pallas_call(functools.partial(kernel, n_site, n_sp), out_shape=tuple((...  41.5 us
    pallas_call x1, Pallas kernels, shards(): pl.pallas_call(write_out, out_shape=out_shape, in_specs=[vmem] * 3, out_s...  1.05 us

profile of v7, /device:TPU:1, one launch (start us, length us, event | category | flops | bytes accessed | tf_op | source)
XLA Modules:
  0.0 43.2 jit_solution(17495365114643696622)
XLA Ops:
  0.6 41.5 %shard_map.112 = (bf16[3584,128]{1,0:T(8,128)(2,1)S(1)}, f32[16,128]{1,0:T(8,128)S(1)}, f32[16,3584]{1,0:T(8,128)S(1)}) custom-call(s32[3584,128]{1,0:T(8,128)} %presence_hbm.1, bf16[3584,128]{1,0:T(8,128)(2,1)} %noise_hbm.1, f32[16,3584]{1,0:T(8,128)} %factors_hbm.1, f32[16,128]{1,0:T(8,128)} %loadings_hbm.1, f32[16,128]{1,0:T(8,128)} %precision_hbm.1, ...), custom_call_target="tpu_custom_call" | custom-call | tf_op jit(solution)/shard_map/pallas_call | solution.py:518
  42.1 1.0 %shard_map.113 = (bf16[3584,128]{1,0:T(8,128)(2,1)}, f32[16,128]{1,0:T(8,128)}, f32[16,3584]{1,0:T(8,128)}) custom-call(bf16[3584,128]{1,0:T(8,128)(2,1)S(1)} %get-tuple-element.6.a, f32[16,128]{1,0:T(8,128)S(1)} %get-tuple-element.7.b, f32[16,3584]{1,0:T(8,128)S(1)} %get-tuple-element.8.c), custom_call_target="tpu_custom_call" | custom-call | tf_op jit(solution)/shard_map/pallas_call | solution.py:564

commit v8 on v7

--- a/solution.py
+++ b/solution.py
@@ -167,7 +167,7 @@
     busy = ny - 1
     rows = factors.shape[1]
     steps = rows // CHUNK
-    cuts = (0, min(2, steps // 2) * CHUNK, steps // 2 * CHUNK, rows)
+    cuts = [CHUNK * (steps * i // 14) for i in (0, 2, 7, 11, 14)]
     species = loadings.shape[1]
 
     site = lax.axis_index("site")
@@ -294,7 +294,7 @@
         return acc + dot(fs[0:32, pl.ds(r0, CHUNK)], pieces, ((1,), (0,)))
 
     acc = jnp.zeros((2 * K, 2 * species), F32)
-    for piece in range(2):
+    for piece in range(3):
         loads[2 + 2 * piece].wait()
         loads[3 + 2 * piece].wait()
         acc = lax.fori_loop(cuts[piece] // CHUNK, cuts[piece + 1] // CHUNK, draw_step, acc, unroll=True)
@@ -324,15 +324,15 @@
         rim.start()
 
 
-    loads[6].wait()
-    loads[7].wait()
-    acc = lax.fori_loop(cuts[2] // CHUNK, steps, draw_step, acc, unroll=True)
+    loads[8].wait()
+    loads[9].wait()
+    acc = lax.fori_loop(cuts[3] // CHUNK, steps, draw_step, acc, unroll=True)
     cross_z[z] = blocks_sum(acc, K, species)
     started += spread_z(cross_z, cz_sems)
     gram_x[x] = gather_z(gram_z, gz_sems)
     started += spread_x(gram_x, gx_sems)
 
-    for load in loads[8:]:
+    for load in loads[10:]:
         load.wait()
     base = site * rows + chunk * CHUNK - RIM
     onehot[...] = jnp.zeros_like(onehot)
@@ -530,7 +530,7 @@
                 pltpu.VMEM((NBR, CHUNK), F32),
                 pltpu.VMEM((rows,), F32),
                 pltpu.VMEM((K, CHUNK), F32),
-                sems((13,)),
+                sems((15,)),
                 pltpu.VMEM((3 * K, rows), BF16),
                 pltpu.VMEM((rows, 2 * species), BF16),
                 pltpu.VMEM((K, RIM + rows), F32),

time: 43.3 us -> 43.9 us (1.014)
  Pallas kernels: 42.5 us -> 43.1 us
    pallas_call x1, Pallas kernels: 41.5 us -> 42 us  [shards(): pl.pallas_call(functools.partial(kernel, n_site, n_sp), out_shape=tuple((...]
where the time goes in v8:
time: 43.9 us; the launch traced here: 43.7 us
  Pallas kernels  43.1 us (98%)
  between operations  0.64 us (1%)
    pallas_call x1, Pallas kernels, shards(): pl.pallas_call(functools.partial(kernel, n_site, n_sp), out_shape=tuple((...  42 us
    pallas_call x1, Pallas kernels, shards(): pl.pallas_call(write_out, out_shape=out_shape, in_specs=[vmem] * 3, out_s...  1.05 us

profile of v8, /device:TPU:1, one launch (start us, length us, event | category | flops | bytes accessed | tf_op | source)
XLA Modules:
  0.0 43.7 jit_solution(3459550370422094653)
XLA Ops:
  0.6 42.0 %shard_map.112 = (bf16[3584,128]{1,0:T(8,128)(2,1)S(1)}, f32[16,128]{1,0:T(8,128)S(1)}, f32[16,3584]{1,0:T(8,128)S(1)}) custom-call(s32[3584,128]{1,0:T(8,128)} %presence_hbm.1, bf16[3584,128]{1,0:T(8,128)(2,1)} %noise_hbm.1, f32[16,3584]{1,0:T(8,128)} %factors_hbm.1, f32[16,128]{1,0:T(8,128)} %loadings_hbm.1, f32[16,128]{1,0:T(8,128)} %precision_hbm.1, ...), custom_call_target="tpu_custom_call" | custom-call | tf_op jit(solution)/shard_map/pallas_call | solution.py:518
  42.7 1.0 %shard_map.113 = (bf16[3584,128]{1,0:T(8,128)(2,1)}, f32[16,128]{1,0:T(8,128)}, f32[16,3584]{1,0:T(8,128)}) custom-call(bf16[3584,128]{1,0:T(8,128)(2,1)S(1)} %get-tuple-element.6.a, f32[16,128]{1,0:T(8,128)S(1)} %get-tuple-element.7.b, f32[16,3584]{1,0:T(8,128)S(1)} %get-tuple-element.8.c), custom_call_target="tpu_custom_call" | custom-call | tf_op jit(solution)/shard_map/pallas_call | solution.py:564

commit v9 on v8

--- a/solution.py
+++ b/solution.py
@@ -167,7 +167,7 @@
     busy = ny - 1
     rows = factors.shape[1]
     steps = rows // CHUNK
-    cuts = [CHUNK * (steps * i // 14) for i in (0, 2, 7, 11, 14)]
+    cuts = [CHUNK * (steps * i // 14) for i in (0, 1, 4, 9, 14)]
     species = loadings.shape[1]
 
     site = lax.axis_index("site")
@@ -434,6 +434,8 @@
         s = ((y + ny - o // CORES) % ny) * CORES + (core + o) % CORES
         remote(lgram_all.at[s], lgram_all.at[s], ly_sems, o, o, {"sp": s}).wait_recv()
 
+    far = (y + ny // 2) % ny
+
     def factors_to(sems, send, recv, index, peer):
         lanes = pl.ds(pl.multiple_of(index * CHUNK, CHUNK), CHUNK)
         return remote(new_factors.at[:, lanes], new_factors.at[:, lanes], sems, send, recv, peer)
@@ -454,6 +456,8 @@
         for d in far_first(ny):
             t = (y + d) % ny
             factors_to(fy_sems, d, y, y * CORES + core, {"sp": t * CORES + core}).start()
+            if d == ny // 2:
+                factors_to(fp_sems, far, y, y * CORES + core, {"sp": far * CORES + (1 - core)}).start()
         factors_to(fp_sems, y, y, y * CORES + core, {"sp": pair}).start()
 
     for copy in started:
@@ -464,7 +468,10 @@
 
         def hand_on():
             factors_to(fy_sems, 0, s, s * CORES + core, {"sp": s * CORES + core}).wait_recv()
-            factors_to(fp_sems, s, s, s * CORES + core, {"sp": pair}).start()
+
+            @pl.when(s != far)
+            def _():
+                factors_to(fp_sems, s, s, s * CORES + core, {"sp": pair}).start()
 
         if e < busy:
             hand_on()
@@ -475,7 +482,14 @@
         factors_to(fp_sems, s, s, s * CORES + (1 - core), {"sp": pair}).wait_recv()
 
     for s in range(busy):
-        factors_to(fp_sems, s, s, s * CORES + core, {"sp": pair}).wait_send()
+
+        @pl.when((s != far) | (y < busy))
+        def _():
+            factors_to(fp_sems, s, s, s * CORES + core, {"sp": pair}).wait_send()
+
+    @pl.when(far == busy)
+    def _():
+        factors_to(fp_sems, far, y, y * CORES + core, {"sp": pair}).wait_send()
 
     @pl.when(y == busy)
     def _():
@@ -553,7 +567,7 @@
                 sems((2, busy)),
                 sems((2, ny)),
                 sems((2, ny)),
-                sems((2, busy)),
+                sems((2, ny)),
             ],
             compiler_params=pltpu.CompilerParams(
                 collective_id=0,

time: 43.9 us -> 44.2 us (level)
  no operation moved by 1% of the time
where the time goes in v9:
time: 44.2 us; the launch traced here: 44.1 us
  Pallas kernels  43.4 us (98%)
  between operations  0.64 us (1%)
    pallas_call x1, Pallas kernels, shards(): pl.pallas_call(functools.partial(kernel, n_site, n_sp), out_shape=tuple((...  42.4 us
    pallas_call x1, Pallas kernels, shards(): pl.pallas_call(write_out, out_shape=out_shape, in_specs=[vmem] * 3, out_s...  1.05 us

profile of v9, /device:TPU:1, one launch (start us, length us, event | category | flops | bytes accessed | tf_op | source)
XLA Modules:
  0.0 44.1 jit_solution(9411719856074311542)
XLA Ops:
  0.6 42.4 %shard_map.112 = (bf16[3584,128]{1,0:T(8,128)(2,1)S(1)}, f32[16,128]{1,0:T(8,128)S(1)}, f32[16,3584]{1,0:T(8,128)S(1)}) custom-call(s32[3584,128]{1,0:T(8,128)} %presence_hbm.1, bf16[3584,128]{1,0:T(8,128)(2,1)} %noise_hbm.1, f32[16,3584]{1,0:T(8,128)} %factors_hbm.1, f32[16,128]{1,0:T(8,128)} %loadings_hbm.1, f32[16,128]{1,0:T(8,128)} %precision_hbm.1, ...), custom_call_target="tpu_custom_call" | custom-call | tf_op jit(solution)/shard_map/pallas_call | solution.py:532
  43.0 1.0 %shard_map.113 = (bf16[3584,128]{1,0:T(8,128)(2,1)}, f32[16,128]{1,0:T(8,128)}, f32[16,3584]{1,0:T(8,128)}) custom-call(bf16[3584,128]{1,0:T(8,128)(2,1)S(1)} %get-tuple-element.6.a, f32[16,128]{1,0:T(8,128)S(1)} %get-tuple-element.7.b, f32[16,3584]{1,0:T(8,128)S(1)} %get-tuple-element.8.c), custom_call_target="tpu_custom_call" | custom-call | tf_op jit(solution)/shard_map/pallas_call | solution.py:578
